TPU v7x, 512 devices: a whole 4x4x16 slice. The times are simulated.
512 devices in a mesh: grp: 4 (over x_lo, core), tile: 128 (over x_hi, z, y).
Axes of the slice: x: 4 (x_hi: 2, x_lo: 2; x = x_hi * 2 + x_lo), y: 4, z: 16, core: 2. Of those that a mesh axis runs over, the one named last changes fastest.
Arguments:
- flow_state: float32 [4, 4, 512, 2048], P('grp', None, 'tile'), may hold values from -6 to 6
- line_owner: int32 [8192, 1], replicated, may hold values from 0 to 127; in each aligned block of 8192 rows (0 to 8191, 8192 to 16383, ...) at most 128 rows name the same one
Outputs:
- record: float32 [4, 128, 512, 128], P('grp', 'tile')
Inputs may be any that keep to these rules, and one draw needn't show every extreme that they name: `line_owner`: no pencil owns more than 128 lines, some pencil owns exactly 128, and every pencil owns at least one line.
All inputs are finite; a program needn't handle non-finite values.
Results may differ from a plain program's by a relative error of at most 0.00002.
Values sent between devices are 32-bit elements; how exact they have to be, the bound alone decides.
No kernel may reach another device: no remote copies, remote signals or barrier semaphores. Data moves between devices by JAX's collectives and lax.ppermute only.
A program may use at most 64 MiB of HBM per device.

v0:
```python
import jax
import jax.numpy as jnp
from jax import lax
from jax.sharding import Mesh
from jax.sharding import PartitionSpec as P

GRP = ("grp_0", "grp_1")


time_step = 0.2
viscosity = 0.05
stencil_reach = 4
first_coeffs = (0.8, -0.2, 4.0 / 105.0, -1.0 / 280.0)
second_center = -205.0 / 72.0
second_coeffs = (1.6, -0.2, 8.0 / 315.0, -1.0 / 560.0)
lift_alpha = -1.586134342059924
lift_beta = -0.052980118572961
lift_gamma = 0.882911075530934
lift_delta = 0.443506852043971
lift_scale = 1.149604398860241


def extended(x, sides, width):
    edges = {}
    for axis, dim in sides:
        devices, length = (lax.axis_size(axis), x.shape[dim])
        up = [(i, (i + 1) % devices) for i in range(devices)]
        last = lax.slice_in_dim(x, length - width, length, axis=dim)
        initial = lax.slice_in_dim(x, 0, width, axis=dim)
        edges[dim] = (
            lax.ppermute(last, axis, up),
            lax.ppermute(initial, axis, [(b, a) for a, b in up]),
        )
    done = []
    for _, dim in sides:
        low, high = edges[dim]
        around = [(width, width) if d in done else (0, 0) for d in range(x.ndim)]
        x = jnp.concatenate([jnp.pad(low, around), x, jnp.pad(high, around)], axis=dim)
        done.append(dim)
    return x


def in_blocks(x, dim, devices):
    before, after = (x.shape[:dim], x.shape[dim + 1 :])
    return jnp.moveaxis(x.reshape(*before, devices, -1, *after), dim, 0)


def in_order(blocks, dim):
    dims = list(blocks.shape[1:])
    dims[dim] *= blocks.shape[0]
    return jnp.moveaxis(blocks, 0, dim).reshape(dims)


def exchange_in_order(blocks, axes, turns):
    dims = [lax.axis_size(a) for a in axes]
    blocks = blocks.reshape(*dims, *blocks.shape[1:])
    for k in turns:
        blocks = lax.all_to_all(blocks, axes[k], split_axis=k, concat_axis=k, tiled=True)
    return blocks.reshape(-1, *blocks.shape[len(axes) :])


def two_step_exchange(x, groups, turns, split_dim, concat_dim):
    devices = lax.axis_size(groups[0]) * lax.axis_size(groups[1])
    blocks = in_blocks(x, split_dim, devices)
    return in_order(exchange_in_order(blocks, groups, turns), concat_dim)


def sent_to_all(x, axis):
    copies = jnp.broadcast_to(x, (lax.axis_size(axis), *x.shape))
    return lax.all_to_all(copies, axis, split_axis=0, concat_axis=0, tiled=True)


def over_copies(x, axis):
    return sent_to_all(x, axis).sum(axis=0)


def first_rolled(field_now, along_axis):
    running = jnp.zeros_like(field_now)
    for offset in range(4):
        forward = jnp.roll(field_now, -(offset + 1), along_axis)
        behind = jnp.roll(field_now, offset + 1, along_axis)
        running = running + first_coeffs[offset] * (forward - behind)
    return running


def second_rolled(field_now, along_axis):
    running = second_center * field_now
    for offset in range(4):
        forward = jnp.roll(field_now, -(offset + 1), along_axis)
        behind = jnp.roll(field_now, offset + 1, along_axis)
        running = running + second_coeffs[offset] * (forward + behind)
    return running


def window_cells(padded, along_axis, offset, rows_here, columns_here):
    row_start = stencil_reach + (offset if along_axis == 1 else 0)
    column_start = stencil_reach + (offset if along_axis == 2 else 0)
    return padded[:, row_start : row_start + rows_here, column_start : column_start + columns_here]


def first_window(padded, along_axis, rows_here, columns_here):
    running = jnp.zeros((padded.shape[0], rows_here, columns_here), jnp.float32)
    for offset in range(4):
        forward = window_cells(padded, along_axis, offset + 1, rows_here, columns_here)
        behind = window_cells(padded, along_axis, -offset - 1, rows_here, columns_here)
        running = running + first_coeffs[offset] * (forward - behind)
    return running


def second_window(padded, along_axis, rows_here, columns_here):
    running = second_center * window_cells(padded, along_axis, 0, rows_here, columns_here)
    for offset in range(4):
        forward = window_cells(padded, along_axis, offset + 1, rows_here, columns_here)
        behind = window_cells(padded, along_axis, -offset - 1, rows_here, columns_here)
        running = running + second_coeffs[offset] * (forward + behind)
    return running


def block_tendencies(fields):
    rows_here = fields.shape[2]
    columns_here = fields.shape[3]
    padded = extended(fields, ((GRP, 3), ("tile", 2)), stencil_reach)
    pressure_padded = padded[3]
    pressure_here = fields[3]
    pressure_grads = (
        first_window(pressure_padded, 1, rows_here, columns_here),
        first_window(pressure_padded, 2, rows_here, columns_here),
        first_rolled(pressure_here, 0),
    )
    result = []
    for component in range(3):
        own_padded = padded[component]
        own_field = fields[component]
        advect = (
            fields[0] * first_window(own_padded, 1, rows_here, columns_here)
            + fields[1] * first_window(own_padded, 2, rows_here, columns_here)
            + fields[2] * first_rolled(own_field, 0)
        )
        laplace = (
            second_window(own_padded, 1, rows_here, columns_here)
            + second_window(own_padded, 2, rows_here, columns_here)
            + second_rolled(own_field, 0)
        )
        result.append(-advect - pressure_grads[component] + viscosity * laplace)
    return jnp.stack(result)


def lift_axis(signal, along_axis):
    length = signal.shape[along_axis]
    even_part = lax.slice_in_dim(signal, 0, length, 2, along_axis)
    odd_part = lax.slice_in_dim(signal, 1, length, 2, along_axis)
    odd_part = odd_part + lift_alpha * (even_part + jnp.roll(even_part, -1, along_axis))
    even_part = even_part + lift_beta * (odd_part + jnp.roll(odd_part, 1, along_axis))
    odd_part = odd_part + lift_gamma * (even_part + jnp.roll(even_part, -1, along_axis))
    even_part = even_part + lift_delta * (odd_part + jnp.roll(odd_part, 1, along_axis))
    return jnp.concatenate([even_part * lift_scale, odd_part / lift_scale], along_axis)


def line_slots(line_owner, pencils, capacity):
    owners = line_owner[:, 0]
    sorted_lines = jnp.argsort(owners, stable=True)
    sorted_owner = owners[sorted_lines]
    targets = jnp.arange(pencils, dtype=jnp.int32)
    starts = jnp.searchsorted(sorted_owner, targets, side="left")
    ends_at = jnp.searchsorted(sorted_owner, targets, side="right")
    counts = ends_at - starts
    slot_index = jnp.arange(capacity, dtype=jnp.int32)
    position = jnp.minimum(starts[:, None] + slot_index[None, :], owners.shape[0] - 1)
    chosen = sorted_lines[position]
    usable = slot_index[None, :] < counts[:, None]
    return (chosen, usable)


def body(flow_state, line_owner):
    group_index = lax.axis_index(GRP)
    fields = two_step_exchange(flow_state, ("grp_0", "grp_1"), (1, 0), 3, 0)
    velocity = fields[:3]
    middle = velocity + time_step * block_tendencies(fields)
    second_fields = jnp.concatenate([middle, fields[3:]], 0)
    quarter = 0.5 * (velocity + middle + time_step * block_tendencies(second_fields))
    outgoing_rows = jnp.concatenate([quarter, jnp.zeros_like(fields[3:])], 0)
    finished = lax.all_to_all(outgoing_rows, GRP, split_axis=0, concat_axis=3, tiled=True)
    coeffs = lift_axis(lift_axis(finished[0], 2), 0)
    planes, rows_here, columns = coeffs.shape
    line_table = jnp.transpose(coeffs, (1, 0, 2)).reshape(rows_here, planes * columns)
    pencils = lax.axis_size("tile")
    capacity = 2 * planes * columns // pencils
    chosen, usable = line_slots(line_owner, pencils, capacity)
    outgoing = jnp.take(line_table, chosen.reshape(-1), axis=1)
    outgoing = jnp.where(usable.reshape(-1)[None, :], outgoing, 0.0)
    received = lax.all_to_all(outgoing, "tile", split_axis=1, concat_axis=0, tiled=True)
    record = lift_axis(received, 0)
    squares = jnp.where(group_index < 3, record * record, 0.0)
    energy = over_copies(squares, GRP)
    return jnp.where(group_index == 3, energy, record)[None, None]


def solution(mesh):
    split = Mesh(mesh.devices.reshape(2, 2, mesh.shape["tile"]), ("grp_0", "grp_1", "tile"))
    in_specs = (P(GRP, None, "tile", None), P())
    out_specs = P(GRP, "tile", None, None)
    return jax.shard_map(body, mesh=split, in_specs=in_specs, out_specs=out_specs, check_vma=False)
```

profile of v0, /device:TPU:6, one launch (start us, length us, event | category | flops | bytes accessed | tf_op | source)
XLA Modules:
  0.0 368.6 jit_solution(12069695524880601099)
XLA Ops:
  1.0 3.8 %all_to_all.46 = f32[2,2,1,4,4,512]{5,0,4,3,2,1:T(2,128)S(1)} all-to-all(f32[2,2,1,4,4,512]{5,0,4,3,2,1:T(2,128)S(1)} %copy.98), channel_id=1, replica_groups=mesh['grp_0'=2,'grp_1'=2,'tile'=128] {'grp_1'}, dimensions={1} | all-to-all | bytes 262144 | tf_op jit(solution)/shard_map/all_to_all | solution.py:58
  5.6 4.2 %all-to-all-start.1 = ((f32[2,2,1,4,4,512]{5,1,4,3,2,0:T(2,128)}), f32[2,2,1,4,4,512]{5,1,4,3,2,0:T(2,128)S(1)}, u32[]{:S(2)}, u32[]{:S(2)}) async-start(f32[2,2,1,4,4,512]{5,1,4,3,2,0:T(2,128)} %copy.99), calls=%async_computation.1 | async-start | bytes 262144 | tf_op jit(solution)/shard_map/all_to_all | solution.py:58
  9.8 7.5 %sort.17 = (s32[8192]{0:T(1024)}, s32[8192]{0:T(1024)S(1)}) sort(s32[8192]{0:T(1024)} %bitcast.203, s32[8192]{0:T(1024)S(1)} %iota.16), dimensions={0}, to_apply=%region_0.1 | sort | flops 106496 | bytes 131072 | tf_op jit(solution)/shard_map/jit(argsort)/sort | solution.py:161
  17.4 45.5 %gather_fusion.2 = s32[8192]{0:T(1024)S(1)} fusion(s32[8192]{0:T(1024)S(1)} %bitcast.204, s32[8192]{0:T(1024)S(1)} %fusion.41), kind=kCustom, calls=%fused_computation.2 | custom fusion | bytes 98304 | tf_op jit(solution)/shard_map/gather | solution.py:162
  62.9 17.0 %while.49 = (s32[]{:T(128)}, u32[128]{0:T(128)S(1)}, u32[128]{0:T(128)S(1)}, s32[8192]{0:T(1024)S(1)}, s32[]{:T(128)}, /*index=5*/s32[]{:T(128)}, s32[]{}) while((s32[]{:T(128)}, u32[128]{0:T(128)S(1)}, u32[128]{0:T(128)S(1)}, s32[8192]{0:T(1024)S(1)}, s32[]{:T(128)}, /*index=5*/s32[]{:T(128)}, s32[]{}) %tuple.114), condition=%wide.region_4.5_spmd.clone, body=%wide.region_3.4_spmd.clone.sunk | while | flops 2692 | bytes 10340 | solution.py:164
  63.0 1.1 gather_fusion.1
  64.2 1.1 gather_fusion.1
  65.4 1.1 gather_fusion.1
  66.6 1.1 gather_fusion.1
  67.8 1.1 gather_fusion.1
  69.0 1.1 gather_fusion.1
  70.3 1.1 gather_fusion.1
  71.5 1.1 gather_fusion.1
  72.7 1.1 gather_fusion.1
  73.9 1.1 gather_fusion.1
  75.1 1.1 gather_fusion.1
  76.3 1.1 gather_fusion.1
  77.6 1.1 gather_fusion.1
  78.8 1.1 gather_fusion.1
  80.0 17.0 %while.48 = (s32[]{:T(128)}, u32[128]{0:T(128)S(1)}, u32[128]{0:T(128)S(1)}, s32[8192]{0:T(1024)S(1)}, s32[]{:T(128)}, /*index=5*/s32[]{:T(128)}, s32[]{}) while((s32[]{:T(128)}, u32[128]{0:T(128)S(1)}, u32[128]{0:T(128)S(1)}, s32[8192]{0:T(1024)S(1)}, s32[]{:T(128)}, /*index=5*/s32[]{:T(128)}, s32[]{}) %tuple.120), condition=%wide.region_2.3_spmd.clone, body=%wide.region_1.2_spmd.clone.sunk | while | flops 2692 | bytes 10340 | solution.py:165
  80.0 1.1 gather_fusion
  81.2 1.1 gather_fusion
  82.4 1.1 gather_fusion
  83.7 1.1 gather_fusion
  97.1 90.5 %gather_fusion.3 = s32[16384]{0:T(1024)S(1)} fusion(s32[8192]{0:T(1024)S(1)} %get-tuple-element.136, s32[16384]{0:T(1024)S(1)} %fusion.22), kind=kCustom, calls=%fused_computation.3 | custom fusion | bytes 196608 | tf_op jit(solution)/shard_map/gather | solution.py:169
  187.9 14.4 %collective-permute-start.3 = (f32[4,4,4,512]{3,2,1,0:T(4,128)S(1)}, f32[4,4,4,512]{3,2,1,0:T(4,128)S(1)}, u32[]{:S(2)}, u32[]{:S(2)}) collective-permute-start(f32[4,4,4,512]{3,2,1,0:T(4,128)S(1)} %bitcast.207), channel_id=1, source_target_pairs={{1,0},{2,1},{3,2},{4,3},{5,4},{6,5},{7,6},{8,7},{9,8},{10,9},{11,1... | collective-permute-start | bytes 393224 | tf_op jit(solution)/shard_map/ppermute | solution.py:32
  202.3 1.9 collective-permute-start
  204.3 1.9 collective-permute-start.1
  206.2 3.6 collective-permute-start.2
  209.9 1.5 collective-permute-done.2
  211.5 3.5 collective-permute-done
  217.0 6.2 %collective-permute-start.7 = (f32[4,4,4,512]{3,2,1,0:T(4,128)S(1)}, f32[4,4,4,512]{3,2,1,0:T(4,128)S(1)}, u32[]{:S(2)}, u32[]{:S(2)}) collective-permute-start(f32[4,4,4,512]{3,2,1,0:T(4,128)S(1)} %pad_maximum_fusion), channel_id=1, source_target_pairs={{1,0},{2,1},{3,2},{4,3},{5,4},{6,5},{7,6},{8,7},{9,8},{10,9},{11,1... | collective-permute-start | bytes 393224 | tf_op jit(solution)/shard_map/ppermute | solution.py:32
  223.1 1.9 collective-permute-start.4
  225.1 1.9 collective-permute-start.5
  227.0 3.6 collective-permute-start.6
  230.7 1.6 collective-permute-done.6
  232.3 3.8 %collective-permute-done.4 = f32[4,4,4,512]{3,2,1,0:T(4,128)S(1)} collective-permute-done((f32[4,4,4,512]{3,2,1,0:T(4,128)S(1)}, f32[4,4,4,512]{3,2,1,0:T(4,128)S(1)}, u32[]{:S(2)}, u32[]{:S(2)}) %collective-permute-start.4) | collective-permute-done | bytes 131104 | tf_op jit(solution)/shard_map/ppermute | solution.py:31
  238.6 3.5 all-to-all-start.2
  242.2 2.7 all-to-all-done.2
  245.1 2.3 slice.1355
  247.4 2.3 slice.1356
  250.8 2.7 copy.102
  253.5 56.9 %gather_fusion.4 = f32[16384,4]{1,0:T(8,128)} fusion(f32[4,8192]{0,1:T(8,128)} %bitcast.218, s32[16384]{0:T(1024)S(1)} %broadcast_clamp_fusion), kind=kCustom, calls=%fused_computation.4 | custom fusion | bytes 589824 | tf_op jit(solution)/shard_map/jit(_take)/gather | solution.py:189
  310.4 5.5 %copy.103 = f32[4,128,128]{2,0,1:T(4,128)S(1)} copy(f32[4,128,128]{0,2,1:T(8,128)} %bitcast.219) | data formatting | bytes 524288 | tf_op jit(solution)/shard_map/jit(_take)/gather | solution.py:189
  316.8 10.0 %all-to-all-start.3 = ((f32[4,128,128]{2,0,1:T(4,128)}), f32[4,128,128]{2,0,1:T(4,128)S(1)}, u32[]{:S(2)}, u32[]{:S(2)}) async-start(f32[4,128,128]{2,0,1:T(4,128)} %select_select_fusion), calls=%async_computation.3 | async-start | bytes 524288 | tf_op jit(solution)/shard_map/all_to_all | solution.py:191
  326.8 22.8 %all-to-all-done.3 = f32[4,128,128]{2,0,1:T(4,128)S(1)} async-done(((f32[4,128,128]{2,0,1:T(4,128)}), f32[4,128,128]{2,0,1:T(4,128)S(1)}, u32[]{:S(2)}, u32[]{:S(2)}) %all-to-all-start.3) | async-done | bytes 262176 | tf_op jit(solution)/shard_map/all_to_all | solution.py:191
  351.1 3.9 %all-to-all-start.4 = ((f32[4,512,128]{2,1,0:T(8,128)}), f32[4,512,128]{2,1,0:T(8,128)S(1)}, u32[]{:S(2)}, u32[]{:S(2)}) async-start(f32[4,512,128]{2,1,0:T(8,128)} %broadcast_in_dim.79), calls=%async_computation.4 | async-start | bytes 2097152 | tf_op jit(solution)/shard_map/all_to_all | solution.py:70
  355.0 12.8 %all-to-all-done.4 = f32[4,512,128]{2,1,0:T(8,128)S(1)} async-done(((f32[4,512,128]{2,1,0:T(8,128)}), f32[4,512,128]{2,1,0:T(8,128)S(1)}, u32[]{:S(2)}, u32[]{:S(2)}) %all-to-all-start.4) | async-done | bytes 1048608 | tf_op jit(solution)/shard_map/all_to_all | solution.py:70
  (180 shorter events, 23.4 us)
Async XLA Ops:
  0.0 17.4 %copy-start = (s32[8192,1]{0,1:T(1,128)S(1)}, s32[8192,1]{0,1:T(1,128)}, u32[]{:S(2)}) copy-start(s32[8192,1]{0,1:T(1,128)} %param.7) | copy-start | bytes 98308
  5.6 182.1 %all-to-all-start.1 = ((f32[2,2,1,4,4,512]{5,1,4,3,2,0:T(2,128)}), f32[2,2,1,4,4,512]{5,1,4,3,2,0:T(2,128)S(1)}, u32[]{:S(2)}, u32[]{:S(2)}) async-start(f32[2,2,1,4,4,512]{5,1,4,3,2,0:T(2,128)} %copy.99), calls=%async_computation.1 | async-start | bytes 262144 | tf_op jit(solution)/shard_map/all_to_all | solution.py:58
  187.9 23.5 %collective-permute-start.3 = (f32[4,4,4,512]{3,2,1,0:T(4,128)S(1)}, f32[4,4,4,512]{3,2,1,0:T(4,128)S(1)}, u32[]{:S(2)}, u32[]{:S(2)}) collective-permute-start(f32[4,4,4,512]{3,2,1,0:T(4,128)S(1)} %bitcast.207), channel_id=1, source_target_pairs={{1,0},{2,1},{3,2},{4,3},{5,4},{6,5},{7,6},{8,7},{9,8},{10,9},{11,1... | collective-permute-start | bytes 393224 | tf_op jit(solution)/shard_map/ppermute | solution.py:32
  202.3 12.6 %collective-permute-start = (f32[4,4,4,512]{3,2,1,0:T(4,128)S(1)}, f32[4,4,4,512]{3,2,1,0:T(4,128)S(1)}, u32[]{:S(2)}, u32[]{:S(2)}) collective-permute-start(f32[4,4,4,512]{3,2,1,0:T(4,128)S(1)} %bitcast.208), channel_id=1, source_target_pairs={{0,1},{1,2},{2,3},{3,4},{4,5},{5,6},{6,7},{7,8},{8,9},{9,10},{10,1... | collective-permute-start | bytes 393224 | tf_op jit(solution)/shard_map/ppermute | solution.py:31
  204.3 5.6 %collective-permute-start.1 = (f32[4,4,4,4]{3,2,1,0:T(4,128)S(1)}, f32[4,4,4,4]{3,2,1,0:T(4,128)S(1)}, u32[]{:S(2)}, u32[]{:S(2)}) collective-permute-start(f32[4,4,4,4]{3,2,1,0:T(4,128)S(1)} %get-tuple-element.237), channel_id=1, source_target_pairs={{0,128},{128,256},{256,384},{384,0},{1,129},{129,257},{257,385},{3... | collective-permute-start | bytes 3080 | tf_op jit(solution)/shard_map/ppermute | solution.py:31
  206.2 5.2 %collective-permute-start.2 = (f32[4,4,4,4]{3,2,1,0:T(4,128)S(1)}, f32[4,4,4,4]{3,2,1,0:T(4,128)S(1)}, u32[]{:S(2)}, u32[]{:S(2)}) collective-permute-start(f32[4,4,4,4]{3,2,1,0:T(4,128)S(1)} %get-tuple-element.238), channel_id=1, source_target_pairs={{128,0},{256,128},{384,256},{0,384},{129,1},{257,129},{385,257},{1... | collective-permute-start | bytes 3080 | tf_op jit(solution)/shard_map/ppermute | solution.py:32
  217.0 15.3 %collective-permute-start.7 = (f32[4,4,4,512]{3,2,1,0:T(4,128)S(1)}, f32[4,4,4,512]{3,2,1,0:T(4,128)S(1)}, u32[]{:S(2)}, u32[]{:S(2)}) collective-permute-start(f32[4,4,4,512]{3,2,1,0:T(4,128)S(1)} %pad_maximum_fusion), channel_id=1, source_target_pairs={{1,0},{2,1},{3,2},{4,3},{5,4},{6,5},{7,6},{8,7},{9,8},{10,9},{11,1... | collective-permute-start | bytes 393224 | tf_op jit(solution)/shard_map/ppermute | solution.py:32
  223.1 12.9 %collective-permute-start.4 = (f32[4,4,4,512]{3,2,1,0:T(4,128)S(1)}, f32[4,4,4,512]{3,2,1,0:T(4,128)S(1)}, u32[]{:S(2)}, u32[]{:S(2)}) collective-permute-start(f32[4,4,4,512]{3,2,1,0:T(4,128)S(1)} %pad_maximum_fusion), channel_id=1, source_target_pairs={{0,1},{1,2},{2,3},{3,4},{4,5},{5,6},{6,7},{7,8},{8,9},{9,10},{10,1... | collective-permute-start | bytes 393224 | tf_op jit(solution)/shard_map/ppermute | solution.py:31
  225.1 5.6 %collective-permute-start.5 = (f32[4,4,4,4]{3,2,1,0:T(4,128)S(1)}, f32[4,4,4,4]{3,2,1,0:T(4,128)S(1)}, u32[]{:S(2)}, u32[]{:S(2)}) collective-permute-start(f32[4,4,4,4]{3,2,1,0:T(4,128)S(1)} %get-tuple-element.211), channel_id=1, source_target_pairs={{0,128},{128,256},{256,384},{384,0},{1,129},{129,257},{257,385},{3... | collective-permute-start | bytes 3080 | tf_op jit(solution)/shard_map/ppermute | solution.py:31
  227.0 5.2 %collective-permute-start.6 = (f32[4,4,4,4]{3,2,1,0:T(4,128)S(1)}, f32[4,4,4,4]{3,2,1,0:T(4,128)S(1)}, u32[]{:S(2)}, u32[]{:S(2)}) collective-permute-start(f32[4,4,4,4]{3,2,1,0:T(4,128)S(1)} %get-tuple-element.212), channel_id=1, source_target_pairs={{128,0},{256,128},{384,256},{0,384},{129,1},{257,129},{385,257},{1... | collective-permute-start | bytes 3080 | tf_op jit(solution)/shard_map/ppermute | solution.py:32
  238.6 6.3 %all-to-all-start.2 = ((f32[4,4,4,512]{3,2,1,0:T(4,128)}), f32[4,4,4,512]{3,2,1,0:T(4,128)S(1)}, u32[]{:S(2)}, u32[]{:S(2)}) async-start(f32[4,4,4,512]{3,2,1,0:T(4,128)} %concatenate.240), calls=%async_computation.2 | async-start | bytes 262144 | tf_op jit(solution)/shard_map/all_to_all | solution.py:182
  316.8 32.8 %all-to-all-start.3 = ((f32[4,128,128]{2,0,1:T(4,128)}), f32[4,128,128]{2,0,1:T(4,128)S(1)}, u32[]{:S(2)}, u32[]{:S(2)}) async-start(f32[4,128,128]{2,0,1:T(4,128)} %select_select_fusion), calls=%async_computation.3 | async-start | bytes 524288 | tf_op jit(solution)/shard_map/all_to_all | solution.py:191
  351.1 16.7 %all-to-all-start.4 = ((f32[4,512,128]{2,1,0:T(8,128)}), f32[4,512,128]{2,1,0:T(8,128)S(1)}, u32[]{:S(2)}, u32[]{:S(2)}) async-start(f32[4,512,128]{2,1,0:T(8,128)} %broadcast_in_dim.79), calls=%async_computation.4 | async-start | bytes 2097152 | tf_op jit(solution)/shard_map/all_to_all | solution.py:70
where the time goes:
time: 374 us; the launch traced here: 369 us
  local copies, waits for them, and re-layouts  242 us (65%)
  starting transfers between devices  57.1 us (15%)
  waiting for transfers between devices  48.7 us (13%)
  other arithmetic  14.8 us (4%)
  blocking collectives  3.84 us (1%)
    gather x1, local copies, waits for them, and re-layouts, line_slots(): chosen = sorted_lines[position]  90.5 us
    gather x2, local copies, waits for them, and re-layouts, body(): outgoing = jnp.take(line_table, chosen.reshape(-1), axis=1)  62.4 us
    gather x1, local copies, waits for them, and re-layouts, line_slots(): sorted_owner = owners[sorted_lines]  45.5 us
    ppermute x4, starting transfers between devices, extended(): lax.ppermute(initial, axis, [(b, a) for a, b in up])  27.8 us
    all_to_all x1, waiting for transfers between devices, body(): lax.all_to_all(outgoing, 'tile', split_axis=1, concat_axis=0, tiled=True)  22.8 us
    gather x14, local copies, waits for them, and re-layouts, line_slots(): starts = jnp.searchsorted(sorted_owner, targets, side='left')  16.1 us
    gather x14, local copies, waits for them, and re-layouts, line_slots(): ends_at = jnp.searchsorted(sorted_owner, targets, side='right')  16.1 us
    all_to_all x1, waiting for transfers between devices, sent_to_all(): return lax.all_to_all(copies, axis, split_axis=0, concat_axis=0, tiled=True)  12.8 us
  transfers between devices with their start and end apart: 12, of which 7 were waited for; matrix products, arithmetic and copies ran while one was open for 48% of the time, Pallas kernels for 0%

commit v1 on v0

v1 whole, which is shorter than its diff:
```python
import jax
import jax.numpy as jnp
from jax import lax
from jax.experimental import pallas as pl
from jax.experimental.pallas import tpu as pltpu
from jax.sharding import Mesh
from jax.sharding import PartitionSpec as P

BLOCK_AXES = ("y", "xl", "co")
LONG_AXES = ("xh", "z")

time_step = 0.2
viscosity = 0.05
first_coeffs = (0.8, -0.2, 4.0 / 105.0, -1.0 / 280.0)
second_center = -205.0 / 72.0
second_coeffs = (1.6, -0.2, 8.0 / 315.0, -1.0 / 560.0)
lift_alpha = -1.586134342059924
lift_beta = -0.052980118572961
lift_gamma = 0.882911075530934
lift_delta = 0.443506852043971
lift_scale = 1.149604398860241

PLANES = 4
CHUNKS = 16
VMEM_LIMIT = 48 * 1024 * 1024


def lanes_of(shape):
    return lax.broadcasted_iota(jnp.int32, shape, len(shape) - 1)


def whole(count):
    return [pl.BlockSpec(memory_space=pltpu.VMEM)] * count


def cost(flops, moved):
    return pl.CostEstimate(flops=flops, bytes_accessed=moved, transcendentals=0)


def pack_kernel(x_ref, out_ref):
    lane = lanes_of((8, 128))
    for c in range(CHUNKS):
        here = slice(128 * c, 128 * c + 128)
        after = slice(128 * ((c + 1) % CHUNKS), 128 * ((c + 1) % CHUNKS) + 128)
        before = slice(128 * ((c - 1) % CHUNKS), 128 * ((c - 1) % CHUNKS) + 128)
        for z in range(PLANES):
            out_ref[c, 4 * z : 4 * z + 4, :] = x_ref[z, :, here]
        right_a = jnp.concatenate([x_ref[0, :, after], x_ref[1, :, after]], 0)
        right_b = jnp.concatenate([x_ref[2, :, after], x_ref[3, :, after]], 0)
        left_a = jnp.concatenate([x_ref[0, :, before], x_ref[1, :, before]], 0)
        left_b = jnp.concatenate([x_ref[2, :, before], x_ref[3, :, before]], 0)
        right = jnp.where(lane < 32, right_a, pltpu.roll(right_b, 32, 1))
        left = jnp.where(lane < 96, pltpu.roll(left_b, 96, 1), left_a)
        out_ref[c, 16:24, :] = jnp.where(lane < 64, right, left)


def pack(x):
    return pl.pallas_call(
        pack_kernel,
        out_shape=jax.ShapeDtypeStruct((CHUNKS, 24, 128), jnp.float32),
        in_specs=whole(1),
        out_specs=whole(1)[0],
        cost_estimate=cost(100_000, 320_000),
        name="pack",
    )(x)


def derivatives(ref, f, z, rows, low):
    here = ref[f, z, low : low + rows, :]
    d_x = d_y = d_z = None
    lap = (3.0 * second_center) * here
    for k in range(1, 5):
        a, e = first_coeffs[k - 1], second_coeffs[k - 1]
        up, down = ref[f, z, low + k : low + k + rows, :], ref[f, z, low - k : low - k + rows, :]
        right, left = pltpu.roll(here, 256 - k, 1), pltpu.roll(here, k, 1)
        over, under = ref[f, (z + k) % 4, low : low + rows, :], ref[f, (z - k) % 4, low : low + rows, :]
        t_x, t_y, t_z = a * (up - down), a * (right - left), a * (over - under)
        d_x = t_x if d_x is None else d_x + t_x
        d_y = t_y if d_y is None else d_y + t_y
        d_z = t_z if d_z is None else d_z + t_z
        lap = lap + e * ((up + down) + (right + left) + (over + under))
    return d_x, d_y, d_z, lap


def pressure_slopes(ref, z, rows, low):
    here = ref[3, z, low : low + rows, :]
    d_x = d_y = d_z = None
    for k in range(1, 5):
        a = first_coeffs[k - 1]
        t_x = a * (ref[3, z, low + k : low + k + rows, :] - ref[3, z, low - k : low - k + rows, :])
        t_y = a * (pltpu.roll(here, 256 - k, 1) - pltpu.roll(here, k, 1))
        t_z = a * (ref[3, (z + k) % 4, low : low + rows, :] - ref[3, (z - k) % 4, low : low + rows, :])
        d_x = t_x if d_x is None else d_x + t_x
        d_y = t_y if d_y is None else d_y + t_y
        d_z = t_z if d_z is None else d_z + t_z
    return d_x, d_y, d_z


def lift_steps(s, odd, axis):
    size = s.shape[axis]
    for coeff, on_odd in ((lift_alpha, True), (lift_beta, False), (lift_gamma, True), (lift_delta, False)):
        step = coeff * (pltpu.roll(s, 1, axis) + pltpu.roll(s, size - 1, axis))
        s = jnp.where(odd == on_odd, s + step, s)
    return s


def flow_kernel(own_ref, low_ref, high_ref, out_ref, fields, middle, lifted):
    lane8 = lanes_of((8, 128))
    for ref, count, base in ((low_ref, 3, 0), (own_ref, 4, 12), (high_ref, 3, 28)):
        for j in range(count):
            for g in range(4):
                block = ref[4 * j + g]
                near = block[16:24]
                far = jnp.where(lane8 < 64, pltpu.roll(near, 96, 1), pltpu.roll(near, 32, 1))
                for z in range(PLANES):
                    rows = slice(base + 4 * j, base + 4 * j + 4)
                    sides = near if z < 2 else far
                    fields[g, z, rows, 0:128] = block[4 * z : 4 * z + 4]
                    fields[g, z, rows, 128:256] = sides[4 * (z % 2) : 4 * (z % 2) + 4]

    for z in range(PLANES):
        slopes = pressure_slopes(fields, z, 32, 4)
        u, v, w = (fields[f, z, 4:36, :] for f in range(3))
        for g in range(3):
            d_x, d_y, d_z, lap = derivatives(fields, g, z, 32, 4)
            tend = viscosity * lap - (u * d_x + v * d_y + w * d_z) - slopes[g]
            middle[g, z, :, :] = (u, v, w)[g] + time_step * tend

    odd_lane = lanes_of((24, 256)) % 2 == 1
    for z in range(PLANES):
        slopes = pressure_slopes(fields, z, 24, 8)
        u, v, w = (middle[f, z, 4:28, :] for f in range(3))
        for g in range(3):
            d_x, d_y, d_z, lap = derivatives(middle, g, z, 24, 4)
            tend = viscosity * lap - (u * d_x + v * d_y + w * d_z) - slopes[g]
            done = 0.5 * ((fields[g, z, 8:32, :] + (u, v, w)[g]) + time_step * tend)
            lifted[g, z, :, :] = lift_steps(done, odd_lane, 1)[:, 0:128]

    odd_row = lax.broadcasted_iota(jnp.int32, (24, 128), 0) % 2 == 1
    for g in range(3):
        even0, odd0, even1, odd1 = (lifted[g, z, :, :] for z in range(PLANES))
        both = lift_alpha * (even0 + even1)
        odd0, odd1 = odd0 + both, odd1 + both
        both = lift_beta * (odd0 + odd1)
        even0, even1 = even0 + both, even1 + both
        both = lift_gamma * (even0 + even1)
        odd0, odd1 = odd0 + both, odd1 + both
        both = lift_delta * (odd0 + odd1)
        even0, even1 = even0 + both, even1 + both
        for z, plane in enumerate((even0, odd0, even1, odd1)):
            lifted[g, z, :, :] = lift_steps(plane, odd_row, 0)

    odd_lane = lanes_of((8, 128)) % 2 == 1
    for z in range(PLANES):
        for half in range(2):
            power = (-1 if z % 2 else 1) + (-1 if half else 1)
            scale = jnp.where(odd_lane, lift_scale ** (power - 1), lift_scale ** (power + 1)).astype(jnp.float32)
            energy = None
            for g in range(3):
                rows = lifted[g, z, pl.ds(4 + half, 8, stride=2), :] * scale
                energy = rows * rows if energy is None else energy + rows * rows
                for copy in range(4):
                    out_ref[copy, g, z, 8 * half : 8 * half + 8, :] = rows
            for copy in range(4):
                out_ref[copy, 3, z, 8 * half : 8 * half + 8, :] = energy


def flow(own, low, high):
    return pl.pallas_call(
        flow_kernel,
        out_shape=jax.ShapeDtypeStruct((4, 4, PLANES, 16, 128), jnp.float32),
        in_specs=whole(3),
        out_specs=whole(1)[0],
        scratch_shapes=[
            pltpu.VMEM((4, PLANES, 40, 256), jnp.float32),
            pltpu.VMEM((3, PLANES, 32, 256), jnp.float32),
            pltpu.VMEM((3, PLANES, 24, 128), jnp.float32),
        ],
        compiler_params=pltpu.CompilerParams(vmem_limit_bytes=VMEM_LIMIT),
        cost_estimate=cost(30_000_000, 1_000_000),
        name="flow",
    )(own, low, high)


def slots_kernel(owner_ref, owner_out, rank_out, rank_rows):
    bf16, f32 = jnp.bfloat16, jnp.float32
    row = lax.broadcasted_iota(jnp.int32, (128, 128), 0)
    lane = lanes_of((128, 128))
    before = jnp.concatenate([(row < lane).astype(f32), jnp.ones((128, 128), f32)], 1).astype(bf16)
    pencil = row
    base = jnp.zeros((128, 128), f32)
    for b in range(64):
        mine = owner_ref[b : b + 1, :] == pencil
        counts = jnp.dot(jnp.where(mine, 1.0, 0.0).astype(bf16), before, preferred_element_type=f32)
        ranks = jnp.where(mine, base + counts[:, 0:128], 0.0)
        rank_rows[b : b + 1, :] = jnp.sum(ranks, axis=0, keepdims=True)
        base = base + counts[:, 128:256]
    owners = owner_ref[...].astype(f32).astype(bf16)
    ranks = rank_rows[...].astype(bf16)
    for part in range(2):
        even = jnp.where(lane == 2 * (row - 64 * part), 1.0, 0.0).astype(bf16)
        odd = jnp.where(lane == 2 * (row - 64 * part) + 1, 1.0, 0.0).astype(bf16)
        for values, out in ((owners, owner_out), (ranks, rank_out)):
            from_even = jnp.dot(values, even, preferred_element_type=f32)
            from_odd = jnp.dot(values, odd, preferred_element_type=f32)
            for z in range(PLANES):
                plane = (0, 2, 1, 3)[z]
                low = from_even[16 * plane : 16 * plane + 8]
                high = from_odd[16 * plane + 8 : 16 * plane + 16]
                out[part, z, :, :] = (low + high).astype(jnp.int32)


def slots(owner_rows):
    shape = jax.ShapeDtypeStruct((2, PLANES, 8, 128), jnp.int32)
    return pl.pallas_call(
        slots_kernel,
        out_shape=(shape, shape),
        in_specs=whole(1),
        out_specs=tuple(whole(2)),
        scratch_shapes=[pltpu.VMEM((64, 128), jnp.float32)],
        compiler_params=pltpu.CompilerParams(vmem_limit_bytes=VMEM_LIMIT),
        cost_estimate=cost(600_000_000, 100_000),
        name="slots",
    )(owner_rows)


def gather_kernel(first_ref, table_ref, owner_ref, rank_ref, out_ref, left):
    bf16, f32 = jnp.bfloat16, jnp.float32
    first = first_ref[0]
    slot = lax.broadcasted_iota(jnp.int32, (128, 128), 0)
    out_ref[...] = jnp.zeros_like(out_ref)

    def chunk(c, carry):
        right = []
        for z in range(PLANES):
            values = table_ref[c, z]
            high = values.astype(bf16).astype(f32)
            low = values - high
            owner = jnp.broadcast_to(owner_ref[c % 2, z, pl.ds(c // 2, 1), :], (16, 128)) - first
            for t in range(32):
                mine = owner == 4 * t
                rows = slice(16 * t, 16 * t + 16)
                left[rows, 256 * z : 256 * z + 128] = jnp.where(mine, high, 0.0).astype(bf16)
                left[rows, 256 * z + 128 : 256 * z + 256] = jnp.where(mine, low, 0.0).astype(bf16)
            rank = rank_ref[c % 2, z, pl.ds(c // 2, 1), :]
            at = jnp.where(rank == slot, 1.0, 0.0).astype(bf16)
            right += [at, at]
        moved = lax.dot_general(
            left[...], jnp.concatenate(right, 1), (((1,), (1,)), ((), ())), preferred_element_type=f32
        )
        out_ref[...] += moved.reshape(32, 16, 128)
        return carry

    lax.fori_loop(0, CHUNKS, chunk, 0)


def gather(first, table, owner, rank):
    return pl.pallas_call(
        gather_kernel,
        out_shape=jax.ShapeDtypeStruct((32, 16, 128), jnp.float32),
        in_specs=[pl.BlockSpec(memory_space=pltpu.SMEM)] + whole(3),
        out_specs=whole(1)[0],
        scratch_shapes=[pltpu.VMEM((512, 1024), jnp.bfloat16)],
        compiler_params=pltpu.CompilerParams(vmem_limit_bytes=VMEM_LIMIT),
        cost_estimate=cost(2_200_000_000, 1_000_000),
        name="gather",
    )(first, table, owner, rank)


def swap(x, axes):
    return lax.all_to_all(x, axes, split_axis=0, concat_axis=0, tiled=True)


def body(flow_state, line_owner):
    owner, rank = slots(line_owner.reshape(64, 128))
    own = swap(pack(flow_state[0]), BLOCK_AXES)
    blocks = lax.axis_size(LONG_AXES)
    up = [(i, (i + 1) % blocks) for i in range(blocks)]
    low = lax.ppermute(own[4:16], LONG_AXES, up)
    high = lax.ppermute(own[0:12], LONG_AXES, [(b, a) for a, b in up])
    coeffs = flow(own, low, high).reshape(16, PLANES, 16, 128)
    table = swap(coeffs, BLOCK_AXES)
    first = lax.axis_index("y").astype(jnp.int32).reshape(1)
    outgoing = gather(first, table, owner, rank)
    record = swap(outgoing, LONG_AXES)
    record = record.reshape(32, 2, 8, 128).transpose(1, 0, 2, 3).reshape(512, 128)
    return record[None, None]


def solution(mesh):
    split = Mesh(mesh.devices.reshape(2, 2, 2, 16, 4), ("xl", "co", "xh", "z", "y"))
    in_specs = (P(("xl", "co"), None, ("xh", "z", "y"), None), P())
    out_specs = P(("xl", "co"), ("xh", "z", "y"), None, None)
    return jax.shard_map(body, mesh=split, in_specs=in_specs, out_specs=out_specs, check_vma=False)
```

time: 374 us -> 96.1 us (0.26)
  the two profiles are of different devices: /device:TPU:6 before, /device:TPU:2 now
where the time goes in v1:
time: 96.1 us; the launch traced here: 95.7 us
  blocking collectives  48.2 us (50%)
  Pallas kernels  18.2 us (19%)
  starting transfers between devices  16.8 us (17%)
  waiting for transfers between devices  11.7 us (12%)
    all_to_all x2, blocking collectives, swap(): return lax.all_to_all(x, axes, split_axis=0, concat_axis=0, tiled=True)  48.2 us
    ppermute x1, starting transfers between devices, body(): high = lax.ppermute(own[0:12], LONG_AXES, [(b, a) for a, b in up])  9.64 us
    all_to_all x1, waiting for transfers between devices, swap(): return lax.all_to_all(x, axes, split_axis=0, concat_axis=0, tiled=True)  8.22 us
    pallas_call x1, Pallas kernels, flow(): pl.pallas_call(flow_kernel, out_shape=jax.ShapeDtypeStruct((4, 4, PLANES,...  7.68 us
    pallas_call x1, Pallas kernels, gather(): pl.pallas_call(gather_kernel, out_shape=jax.ShapeDtypeStruct((32, 16, 128...  7.3 us
    all_to_all x1, starting transfers between devices, swap(): return lax.all_to_all(x, axes, split_axis=0, concat_axis=0, tiled=True)  5.2 us
    ppermute x1, waiting for transfers between devices, body(): low = lax.ppermute(own[4:16], LONG_AXES, up)  2.32 us
  transfers between devices with their start and end apart: 3, of which 3 were waited for; matrix products, arithmetic and copies ran while one was open for 0% of the time, Pallas kernels for 2%

profile of v1, /device:TPU:2, one launch (start us, length us, event | category | flops | bytes accessed | tf_op | source)
XLA Modules:
  0.0 95.7 jit_solution(12567691911499688354)
XLA Ops:
  0.0 1.7 %pack.1 = f32[16,24,128]{2,1,0:T(8,128)} custom-call(f32[4,4,2048]{2,1,0:T(4,128)} %bitcast.10), custom_call_target="tpu_custom_call" | custom-call | flops 100000 | bytes 320000 | tf_op jit(solution)/shard_map/pack/pallas_call | solution.py:58
  1.7 15.1 %all_to_all.15.own_ref = f32[16,24,128]{2,1,0:T(8,128)S(1)} all-to-all(f32[16,24,128]{2,1,0:T(8,128)} %pack.1), channel_id=1, replica_groups=mesh['xl'=2,'co'=2,'xh'=2,'z'=16,'y'=4] {'y','xl','co'}, dimensions={0} | all-to-all | bytes 393216 | tf_op jit(solution)/shard_map/all_to_all | solution.py:271
  16.8 1.9 %collective-permute-start = (f32[12,24,128]{2,1,0:T(8,128)S(1)}, f32[12,24,128]{2,1,0:T(8,128)S(1)}, u32[]{:S(2)}, u32[]{:S(2)}) collective-permute-start(f32[12,24,128]{2,1,0:T(8,128)S(1)} %get-tuple-element.10), channel_id=1, source_target_pairs={{0,4},{4,8},{8,12},{12,16},{16,20},{20,24},{24,28},{28,32},{32,36}... | collective-permute-start | bytes 442376 | tf_op jit(solution)/shard_map/ppermute | solution.py:279
  18.7 9.6 %collective-permute-start.1 = (f32[12,24,128]{2,1,0:T(8,128)S(1)}, f32[12,24,128]{2,1,0:T(8,128)S(1)}, u32[]{:S(2)}, u32[]{:S(2)}) collective-permute-start(f32[12,24,128]{2,1,0:T(8,128)S(1)} %get-tuple-element.9), channel_id=1, source_target_pairs={{4,0},{8,4},{12,8},{16,12},{20,16},{24,20},{28,24},{32,28},{36,32}... | collective-permute-start | bytes 442376 | tf_op jit(solution)/shard_map/ppermute | solution.py:280
  28.4 2.3 %collective-permute-done.low_ref = f32[12,24,128]{2,1,0:T(8,128)S(1)} collective-permute-done((f32[12,24,128]{2,1,0:T(8,128)S(1)}, f32[12,24,128]{2,1,0:T(8,128)S(1)}, u32[]{:S(2)}, u32[]{:S(2)}) %collective-permute-start) | collective-permute-done | bytes 147488 | tf_op jit(solution)/shard_map/ppermute | solution.py:279
  30.7 1.2 %collective-permute-done.1.high_ref = f32[12,24,128]{2,1,0:T(8,128)S(1)} collective-permute-done((f32[12,24,128]{2,1,0:T(8,128)S(1)}, f32[12,24,128]{2,1,0:T(8,128)S(1)}, u32[]{:S(2)}, u32[]{:S(2)}) %collective-permute-start.1) | collective-permute-done | bytes 147488 | tf_op jit(solution)/shard_map/ppermute | solution.py:280
  31.9 7.7 %flow.1 = f32[4,4,4,16,128]{4,3,2,1,0:T(8,128)} custom-call(f32[16,24,128]{2,1,0:T(8,128)S(1)} %all_to_all.15.own_ref, f32[12,24,128]{2,1,0:T(8,128)S(1)} %collective-permute-done.low_ref, f32[12,24,128]{2,1,0:T(8,128)S(1)} %collective-permute-done.1.high_ref), custom_call_target="tpu_custom_call" | custom-call | flops 30000000 | bytes 1000000 | tf_op jit(solution)/shard_map/flow/pallas_call | solution.py:169
  39.6 0.0 copy-start
  39.6 5.2 %all-to-all-start.1 = ((f32[16,4,16,128]{3,2,1,0:T(8,128)}), f32[16,4,16,128]{3,2,1,0:T(8,128)S(1)}, u32[]{:S(2)}, u32[]{:S(2)}) async-start(f32[16,4,16,128]{3,2,1,0:T(8,128)} %bitcast.2), calls=%async_computation.1 | async-start | bytes 1048576 | tf_op jit(solution)/shard_map/all_to_all | solution.py:271
  44.8 0.0 copy-done
  44.8 1.5 %slots.1 = (s32[2,4,8,128]{3,2,1,0:T(8,128)S(1)}, s32[2,4,8,128]{3,2,1,0:T(8,128)S(1)}) custom-call(s32[64,128]{1,0:T(8,128)S(1)} %bitcast.8), custom_call_target="tpu_custom_call" | custom-call | flops 600000000 | bytes 100000 | tf_op jit(solution)/shard_map/slots/pallas_call | solution.py:215
  46.3 8.2 %all-to-all-done.1.table_ref = f32[16,4,16,128]{3,2,1,0:T(8,128)S(1)} async-done(((f32[16,4,16,128]{3,2,1,0:T(8,128)}), f32[16,4,16,128]{3,2,1,0:T(8,128)S(1)}, u32[]{:S(2)}, u32[]{:S(2)}) %all-to-all-start.1) | async-done | bytes 524320 | tf_op jit(solution)/shard_map/all_to_all | solution.py:271
  54.6 7.3 %gather.1 = f32[32,16,128]{2,1,0:T(8,128)S(1)} custom-call(s32[1]{0:T(128)} %bitcast.first_ref, f32[16,4,16,128]{3,2,1,0:T(8,128)S(1)} %all-to-all-done.1.table_ref, s32[2,4,8,128]{3,2,1,0:T(8,128)S(1)} %get-tuple-element.7.owner_ref, s32[2,4,8,128]{3,2,1,0:T(8,128)S(1)} %get-tuple-element.8.rank_ref), custom_call_target="tpu_custom_call" | custom-call | flops 2200000000 | bytes 1000000 | tf_op jit(solution)/shard_map/gather/pallas_call | solution.py:258
  61.9 33.1 %all_to_all.16 = f32[32,16,128]{2,1,0:T(8,128)S(1)} all-to-all(f32[32,16,128]{2,1,0:T(8,128)S(1)} %gather.1), channel_id=1, replica_groups=mesh['xl'=2,'co'=2,'xh'=2,'z'=16,'y'=4] {'xh','z'}, dimensions={0} | all-to-all | bytes 524288 | tf_op jit(solution)/shard_map/all_to_all | solution.py:271
  95.0 0.7 copy.3
  (1 shorter events, 0.0 us)
Async XLA Ops:
  16.8 13.9 %collective-permute-start = (f32[12,24,128]{2,1,0:T(8,128)S(1)}, f32[12,24,128]{2,1,0:T(8,128)S(1)}, u32[]{:S(2)}, u32[]{:S(2)}) collective-permute-start(f32[12,24,128]{2,1,0:T(8,128)S(1)} %get-tuple-element.10), channel_id=1, source_target_pairs={{0,4},{4,8},{8,12},{12,16},{16,20},{20,24},{24,28},{28,32},{32,36}... | collective-permute-start | bytes 442376 | tf_op jit(solution)/shard_map/ppermute | solution.py:279
  18.7 13.2 %collective-permute-start.1 = (f32[12,24,128]{2,1,0:T(8,128)S(1)}, f32[12,24,128]{2,1,0:T(8,128)S(1)}, u32[]{:S(2)}, u32[]{:S(2)}) collective-permute-start(f32[12,24,128]{2,1,0:T(8,128)S(1)} %get-tuple-element.9), channel_id=1, source_target_pairs={{4,0},{8,4},{12,8},{16,12},{20,16},{24,20},{28,24},{32,28},{36,32}... | collective-permute-start | bytes 442376 | tf_op jit(solution)/shard_map/ppermute | solution.py:280
  39.6 5.2 %copy-start = (s32[8192,1]{0,1:T(1,128)S(1)}, s32[8192,1]{0,1:T(1,128)}, u32[]{:S(2)}) copy-start(s32[8192,1]{0,1:T(1,128)} %param.3) | copy-start | bytes 98308
  39.6 15.0 %all-to-all-start.1 = ((f32[16,4,16,128]{3,2,1,0:T(8,128)}), f32[16,4,16,128]{3,2,1,0:T(8,128)S(1)}, u32[]{:S(2)}, u32[]{:S(2)}) async-start(f32[16,4,16,128]{3,2,1,0:T(8,128)} %bitcast.2), calls=%async_computation.1 | async-start | bytes 1048576 | tf_op jit(solution)/shard_map/all_to_all | solution.py:271

commit v2 on v1

v2 whole, which is shorter than its diff:
```python
import jax
import jax.numpy as jnp
from jax import lax
from jax.experimental import pallas as pl
from jax.experimental.pallas import tpu as pltpu
from jax.sharding import Mesh
from jax.sharding import PartitionSpec as P

BLOCK_AXES = ("y", "xl", "co")
LONG_AXES = ("xh", "z")

time_step = 0.2
viscosity = 0.05
first_coeffs = (0.8, -0.2, 4.0 / 105.0, -1.0 / 280.0)
second_center = -205.0 / 72.0
second_coeffs = (1.6, -0.2, 8.0 / 315.0, -1.0 / 560.0)
lift_alpha = -1.586134342059924
lift_beta = -0.052980118572961
lift_gamma = 0.882911075530934
lift_delta = 0.443506852043971
lift_scale = 1.149604398860241

PLANES = 4
CHUNKS = 16
VMEM_LIMIT = 24 * 1024 * 1024


def lanes_of(shape):
    return lax.broadcasted_iota(jnp.int32, shape, len(shape) - 1)


def whole(count):
    return [pl.BlockSpec(memory_space=pltpu.VMEM)] * count


def cost(flops, moved):
    return pl.CostEstimate(flops=flops, bytes_accessed=moved, transcendentals=0)


def pack_kernel(x_ref, out_ref):
    right_lane = lanes_of((4, 128)) < 64
    for r in range(4):
        chunks = [x_ref[:, r, 128 * c : 128 * c + 128] for c in range(CHUNKS)]
        for c in range(CHUNKS):
            out_ref[c, r, 0:4, :] = chunks[c]
            out_ref[c, r, 4:8, :] = jnp.where(right_lane, chunks[(c + 1) % CHUNKS], chunks[c - 1])


def pack(x):
    return pl.pallas_call(
        pack_kernel,
        out_shape=pltpu.VMEM((CHUNKS, 4, 8, 128), jnp.float32),
        in_specs=whole(1),
        out_specs=whole(1)[0],
        cost_estimate=cost(100_000, 400_000),
        name="pack",
    )(x)


def folded(coeffs, sign):
    weights = [0.0] * PLANES
    for k, value in enumerate(coeffs, 1):
        weights[k % PLANES] += value
        weights[-k % PLANES] += sign * value
    return weights


def column_shifts(here, lane, reach):
    other = pltpu.roll(here, 4, 1)
    right = [pltpu.roll(jnp.where(lane < k, other, here), 128 - k, 2) for k in range(1, reach + 1)]
    left = [pltpu.roll(jnp.where(lane >= 128 - k, other, here), k, 2) for k in range(1, reach + 1)]
    return right, left


def plane_shifts(here, plane):
    over = jnp.where(plane < 3, pltpu.roll(here, 7, 1), pltpu.roll(here, 3, 1))
    under = jnp.where(plane > 0, pltpu.roll(here, 1, 1), pltpu.roll(here, 5, 1))
    return over, under


def plane_opposite(here, plane):
    return jnp.where(plane < 2, pltpu.roll(here, 6, 1), pltpu.roll(here, 2, 1))


def weighted(coeffs, terms):
    total = None
    for value, term in zip(coeffs, terms):
        total = value * term if total is None else total + value * term
    return total


def derivatives(load, low, lane, plane, second=True):
    here = load(low)
    right, left = column_shifts(here, lane, 4)
    up, down = ([load(low + s * k) for k in range(1, 5)] for s in (1, -1))
    over, under = plane_shifts(here, plane)
    _, forward, _, behind = folded(first_coeffs, -1.0)
    assert forward == -behind
    d_x = weighted(first_coeffs, [a - b for a, b in zip(up, down)])
    d_y = weighted(first_coeffs, [a - b for a, b in zip(right, left)])
    d_z = forward * (over - under)
    if not second:
        return d_x, d_y, d_z
    centre, near, far, _ = folded(second_coeffs, 1.0)
    lap = weighted(second_coeffs, [(a + b) + (c + d) for a, b, c, d in zip(up, down, right, left)])
    lap = lap + (3.0 * second_center + centre) * here
    lap = lap + (near * (over + under) + far * plane_opposite(here, plane))
    return d_x, d_y, d_z, lap


def flow_kernel(own_ref, low_ref, high_ref, out_ref, fields, middle, slopes, lifted):
    for ref, count, base in ((low_ref, 3, 0), (own_ref, 4, 12), (high_ref, 3, 28)):
        for j in range(count):
            for g in range(4):
                fields[g, base + 4 * j : base + 4 * j + 4] = ref[4 * j + g]

    shape = (4, 8, 128)
    lane = lanes_of(shape)
    plane = lax.broadcasted_iota(jnp.int32, shape, 1) % 4

    def loader(ref, g):
        return lambda low: ref[g, pl.ds(low, 4)]

    def first(i, carry):
        low = 4 + 4 * i
        grads = derivatives(loader(fields, 3), low, lane, plane, second=False)
        u, v, w = (fields[f, pl.ds(low, 4)] for f in range(3))
        for g in range(3):
            d_x, d_y, d_z, lap = derivatives(loader(fields, g), low, lane, plane)
            slopes[g, pl.ds(4 * i, 4)] = grads[g]
            tend = viscosity * lap - (u * d_x + v * d_y + w * d_z) - grads[g]
            middle[g, pl.ds(4 * i, 4)] = (u, v, w)[g] + time_step * tend
        return carry

    lax.fori_loop(0, 8, first, 0)

    def second(i, carry):
        low = 4 + 4 * i
        u, v, w = (middle[f, pl.ds(low, 4)] for f in range(3))
        for g in range(3):
            d_x, d_y, d_z, lap = derivatives(loader(middle, g), low, lane, plane)
            tend = viscosity * lap - (u * d_x + v * d_y + w * d_z) - slopes[g, pl.ds(low, 4)]
            s = 0.5 * ((fields[g, pl.ds(low + 4, 4)] + (u, v, w)[g]) + time_step * tend)
            lifted[g, pl.ds(4 * i, 4)] = s
        return carry

    lax.fori_loop(0, 6, second, 0)

    lane, sub = lanes_of((8, 128)), lax.broadcasted_iota(jnp.int32, (8, 128), 0)
    odd_y, odd_z, first_row = lane % 2 == 1, sub % 2 == 1, sub < 4

    def chosen(odd, pair):
        return jnp.where(odd, jnp.float32(pair[1]), jnp.float32(pair[0]))

    taps = [chosen(odd_y, pair) for pair in filter_taps(None)]
    same, opposite = (chosen(odd_z, pair) for pair in filter_taps(PLANES))
    energy = [None] * 8
    for g in range(3):
        even = [lifted[g, 2 * i] for i in range(12)]
        odd = [lifted[g, 2 * i + 1] for i in range(12)]
        odd = [o + lift_alpha * (even[i] + even[i + 1]) for i, o in enumerate(odd[:11])]
        even = [None] + [even[i] + lift_beta * (odd[i] + odd[i - 1]) for i in range(1, 11)]
        odd = [None] + [odd[i] + lift_gamma * (even[i] + even[i + 1]) for i in range(1, 10)]
        even = [None, None] + [even[i] + lift_delta * (odd[i] + odd[i - 1]) for i in range(2, 10)]
        for pair in range(8):
            a, b = (even, odd)[pair // 4][2 + 2 * (pair % 4) : 4 + 2 * (pair % 4)]
            here = jnp.where(first_row, a, pltpu.roll(b, 4, 0))
            around = jnp.where(first_row, pltpu.roll(a, 4, 0), b)
            rows = taps[0] * here
            for k in range(1, 5):
                right = pltpu.roll(jnp.where(lane < k, around, here), 128 - k, 1)
                left = pltpu.roll(jnp.where(lane >= 128 - k, around, here), k, 1)
                rows = rows + taps[k] * (right + left)
            both = rows + jnp.where(sub % 4 < 2, pltpu.roll(rows, 6, 0), pltpu.roll(rows, 2, 0))
            others = jnp.where(odd_z, pltpu.roll(both, 1, 0), pltpu.roll(both, 7, 0))
            rows = rows + (same * both + opposite * others)
            scale = chosen(odd_z, (lift_scale, 1.0 / lift_scale)) * (lift_scale if pair < 4 else 1.0 / lift_scale)
            rows = rows * scale
            energy[pair] = rows * rows if g == 0 else energy[pair] + rows * rows
            for copy in range(4):
                out_ref[4 * copy + g, 8 * pair : 8 * pair + 8, :] = rows
    for pair in range(8):
        for copy in range(4):
            out_ref[4 * copy + 3, 8 * pair : 8 * pair + 8, :] = energy[pair]


def filter_taps(ring):
    size = ring or 32

    def lifted(s):
        for value, start in ((lift_alpha, 1), (lift_beta, 0), (lift_gamma, 1), (lift_delta, 0)):
            s = list(s)
            for i in range(start, size, 2):
                s[i] += value * (s[i - 1] + s[(i + 1) % size])
        return s

    answers = [lifted([1.0 if i == j else 0.0 for i in range(size)]) for j in range(size)]
    if ring:
        return tuple(tuple(answers[(i + d) % size][i] - (0.0 if d else 1.0) for i in (0, 1)) for d in (0, 1))
    scales = (lift_scale, 1.0 / lift_scale)
    return [tuple(answers[16 + odd + k][16 + odd] * scales[odd] for odd in (0, 1)) for k in range(5)]


def flow(own, low, high):
    return pl.pallas_call(
        flow_kernel,
        out_shape=pltpu.VMEM((16, 64, 128), jnp.float32),
        in_specs=whole(3),
        out_specs=whole(1)[0],
        scratch_shapes=[
            pltpu.VMEM((4, 40, 8, 128), jnp.float32),
            pltpu.VMEM((3, 32, 8, 128), jnp.float32),
            pltpu.VMEM((3, 32, 8, 128), jnp.float32),
            pltpu.VMEM((3, 24, 8, 128), jnp.float32),
        ],
        compiler_params=pltpu.CompilerParams(vmem_limit_bytes=VMEM_LIMIT),
        cost_estimate=cost(30_000_000, 1_000_000),
        name="flow",
    )(own, low, high)


def slots_kernel(owner_ref, owner_out, rank_out, rank_rows):
    bf16, f32 = jnp.bfloat16, jnp.float32
    row = lax.broadcasted_iota(jnp.int32, (128, 128), 0)
    lane = lanes_of((128, 128))
    before = jnp.concatenate([(row < lane).astype(f32), jnp.ones((128, 128), f32)], 1).astype(bf16)
    pencil = row
    base = jnp.zeros((128, 128), f32)
    for b in range(64):
        mine = owner_ref[b : b + 1, :] == pencil
        counts = jnp.dot(jnp.where(mine, 1.0, 0.0).astype(bf16), before, preferred_element_type=f32)
        ranks = jnp.where(mine, base + counts[:, 0:128], 0.0)
        rank_rows[b : b + 1, :] = jnp.sum(ranks, axis=0, keepdims=True)
        base = base + counts[:, 128:256]
    owners = owner_ref[...].astype(f32).astype(bf16)
    ranks = rank_rows[...].astype(bf16)
    for part in range(2):
        even = jnp.where(lane == 2 * (row - 64 * part), 1.0, 0.0).astype(bf16)
        odd = jnp.where(lane == 2 * (row - 64 * part) + 1, 1.0, 0.0).astype(bf16)
        for values, out in ((owners, owner_out), (ranks, rank_out)):
            from_even = jnp.dot(values, even, preferred_element_type=f32)
            from_odd = jnp.dot(values, odd, preferred_element_type=f32)
            for z in range(PLANES):
                plane = (0, 2, 1, 3)[z]
                low = from_even[16 * plane : 16 * plane + 8]
                high = from_odd[16 * plane + 8 : 16 * plane + 16]
                out[part, z, :, :] = (low + high).astype(jnp.int32)


def slots(owner_rows):
    shape = jax.ShapeDtypeStruct((2, PLANES, 8, 128), jnp.int32)
    return pl.pallas_call(
        slots_kernel,
        out_shape=(shape, shape),
        in_specs=whole(1),
        out_specs=tuple(whole(2)),
        scratch_shapes=[pltpu.VMEM((64, 128), jnp.float32)],
        compiler_params=pltpu.CompilerParams(vmem_limit_bytes=VMEM_LIMIT),
        cost_estimate=cost(600_000_000, 100_000),
        name="slots",
    )(owner_rows)


def gather_kernel(first_ref, table_ref, owner_ref, rank_ref, out_ref):
    bf16, f32 = jnp.bfloat16, jnp.float32
    first = first_ref[0]
    slot = lax.broadcasted_iota(jnp.int32, (256, 128), 0).astype(f32).astype(bf16)
    nothing = jnp.zeros((16, 128), bf16)

    def spread(row, rows):
        return jnp.broadcast_to(row, (rows, 128)).astype(f32).astype(bf16)

    def chunk(c, carry):
        moved = None
        for z in range(PLANES):
            values = table_ref[c, pl.ds(z, 16, stride=4), :]
            high = values.astype(bf16)
            low = (values - high.astype(f32)).astype(bf16)
            owner = owner_ref[c % 2, z, pl.ds(c // 2, 1), :]
            rank = rank_ref[c % 2, z, pl.ds(c // 2, 1), :]
            mine = owner % 4 == first
            pencil = owner // 4
            lower = spread(jnp.where(mine, pencil % 16, -1), 16)
            at = spread(jnp.where(mine, 128 * (pencil // 16) + rank, -1), 16)
            left = []
            for t in range(16):
                hit = lower == jnp.asarray(t, bf16)
                left.append(jnp.concatenate([jnp.where(hit, high, nothing), jnp.where(hit, low, nothing)], 1))
            ones = jnp.ones((16, 128), bf16)
            right = [jnp.where(at == slot[16 * k : 16 * k + 16], ones, nothing) for k in range(16)]
            right = jnp.concatenate(right, 0)
            part = lax.dot_general(
                jnp.concatenate(left, 0),
                jnp.concatenate([right, right], 1),
                (((1,), (1,)), ((), ())),
                preferred_element_type=f32,
            )
            moved = part if moved is None else moved + part
        for upper in range(2):
            part = moved[:, 128 * upper : 128 * upper + 128].reshape(16, 16, 128)
            rows = slice(16 * upper, 16 * upper + 16)
            out_ref[rows] = jnp.where(c == 0, part, out_ref[rows] + part)
        return carry

    lax.fori_loop(0, CHUNKS, chunk, 0, unroll=4)


def gather(first, table, owner, rank):
    return pl.pallas_call(
        gather_kernel,
        out_shape=jax.ShapeDtypeStruct((32, 16, 128), jnp.float32),
        in_specs=[pl.BlockSpec(memory_space=pltpu.SMEM)] + whole(3),
        out_specs=whole(1)[0],
        compiler_params=pltpu.CompilerParams(vmem_limit_bytes=VMEM_LIMIT),
        cost_estimate=cost(2_200_000_000, 1_000_000),
        name="gather",
    )(first, table, owner, rank)


def swap(x, axes):
    return lax.all_to_all(x, axes, split_axis=0, concat_axis=0, tiled=True)


def body(flow_state, line_owner):
    own = swap(pack(flow_state[0]), BLOCK_AXES)
    blocks = lax.axis_size(LONG_AXES)
    up = [(i, (i + 1) % blocks) for i in range(blocks)]
    own, lines = lax.optimization_barrier((own, line_owner.reshape(64, 128)))
    low = lax.ppermute(own[4:16], LONG_AXES, up)
    high = lax.ppermute(own[0:12], LONG_AXES, [(b, a) for a, b in up])
    owner, rank = slots(lines)
    own, owner, rank = lax.optimization_barrier((own, owner, rank))
    table = swap(flow(own, low, high), BLOCK_AXES)
    first = lax.axis_index("y").astype(jnp.int32).reshape(1)
    outgoing = gather(first, table, owner, rank)
    record = swap(outgoing, LONG_AXES)
    record = record.reshape(32, 2, 8, 128).transpose(1, 0, 2, 3).reshape(512, 128)
    return record[None, None]


def solution(mesh):
    split = Mesh(mesh.devices.reshape(2, 2, 2, 16, 4), ("xl", "co", "xh", "z", "y"))
    in_specs = (P(("xl", "co"), None, ("xh", "z", "y"), None), P())
    out_specs = P(("xl", "co"), ("xh", "z", "y"), None, None)
    return jax.shard_map(body, mesh=split, in_specs=in_specs, out_specs=out_specs, check_vma=False)
```

time: 96.1 us -> 88.8 us (0.924)
  Pallas kernels: 18.2 us -> 9.69 us
    pallas_call x2, Pallas kernels: 9.37 us -> 5.02 us  [the longest x1 4.02 us: flow(): pl.pallas_call(flow_kernel, out_shape=pltpu.VMEM((16, 64, 128), jnp.float...]
    pallas_call x1, Pallas kernels: 7.3 us -> 3.11 us  [gather(): pl.pallas_call(gather_kernel, out_shape=jax.ShapeDtypeStruct((32, 16, 128...]
    all_to_all x1, waiting for transfers between devices: 8.22 us -> 9.78 us  [swap(): return lax.all_to_all(x, axes, split_axis=0, concat_axis=0, tiled=True)]
where the time goes in v2:
time: 88.8 us; the launch traced here: 88.4 us
  blocking collectives  48.3 us (54%)
  starting transfers between devices  17 us (19%)
  waiting for transfers between devices  12.6 us (14%)
  Pallas kernels  9.69 us (11%)
    all_to_all x2, blocking collectives, swap(): return lax.all_to_all(x, axes, split_axis=0, concat_axis=0, tiled=True)  48.3 us
    ppermute x1, starting transfers between devices, body(): high = lax.ppermute(own[0:12], LONG_AXES, [(b, a) for a, b in up])  10.3 us
    all_to_all x1, waiting for transfers between devices, swap(): return lax.all_to_all(x, axes, split_axis=0, concat_axis=0, tiled=True)  9.78 us
    all_to_all x1, starting transfers between devices, swap(): return lax.all_to_all(x, axes, split_axis=0, concat_axis=0, tiled=True)  4.75 us
    pallas_call x1, Pallas kernels, flow(): pl.pallas_call(flow_kernel, out_shape=pltpu.VMEM((16, 64, 128), jnp.float...  4.02 us
    pallas_call x1, Pallas kernels, gather(): pl.pallas_call(gather_kernel, out_shape=jax.ShapeDtypeStruct((32, 16, 128...  3.11 us
    ppermute x1, starting transfers between devices, body(): low = lax.ppermute(own[4:16], LONG_AXES, up)  1.92 us
  transfers between devices with their start and end apart: 3, of which 3 were waited for; matrix products, arithmetic and copies ran while one was open for 0% of the time, Pallas kernels for 2%

profile of v2, /device:TPU:2, one launch (start us, length us, event | category | flops | bytes accessed | tf_op | source)
XLA Modules:
  0.0 88.4 jit_solution(2923601140866191283)
XLA Ops:
  0.0 1.0 %pack.1 = f32[16,4,8,128]{3,2,1,0:T(8,128)S(1)} custom-call(f32[4,4,2048]{2,1,0:T(4,128)} %bitcast.9), custom_call_target="tpu_custom_call" | custom-call | flops 100000 | bytes 400000 | tf_op jit(solution)/shard_map/pack/pallas_call | solution.py:50
  1.0 15.2 %all_to_all.15.own_ref = f32[16,4,8,128]{3,2,1,0:T(8,128)S(1)} all-to-all(f32[16,4,8,128]{3,2,1,0:T(8,128)S(1)} %pack.1), channel_id=1, replica_groups=mesh['xl'=2,'co'=2,'xh'=2,'z'=16,'y'=4] {'y','xl','co'}, dimensions={0} | all-to-all | bytes 524288 | tf_op jit(solution)/shard_map/all_to_all | solution.py:321
  16.2 0.0 copy-start
  16.2 1.9 %collective-permute-start = (f32[12,4,8,128]{3,2,1,0:T(8,128)S(1)}, f32[12,4,8,128]{3,2,1,0:T(8,128)S(1)}, u32[]{:S(2)}, u32[]{:S(2)}) collective-permute-start(f32[12,4,8,128]{3,2,1,0:T(8,128)S(1)} %get-tuple-element.20), channel_id=1, source_target_pairs={{0,4},{4,8},{8,12},{12,16},{16,20},{20,24},{24,28},{28,32},{32,36}... | collective-permute-start | bytes 589832 | tf_op jit(solution)/shard_map/ppermute | solution.py:329
  18.1 10.3 %collective-permute-start.1 = (f32[12,4,8,128]{3,2,1,0:T(8,128)S(1)}, f32[12,4,8,128]{3,2,1,0:T(8,128)S(1)}, u32[]{:S(2)}, u32[]{:S(2)}) collective-permute-start(f32[12,4,8,128]{3,2,1,0:T(8,128)S(1)} %get-tuple-element.19), channel_id=1, source_target_pairs={{4,0},{8,4},{12,8},{16,12},{20,16},{24,20},{28,24},{32,28},{36,32}... | collective-permute-start | bytes 589832 | tf_op jit(solution)/shard_map/ppermute | solution.py:330
  28.5 0.0 copy-done
  28.5 1.6 %slots.1 = (s32[2,4,8,128]{3,2,1,0:T(8,128)S(1)}, s32[2,4,8,128]{3,2,1,0:T(8,128)S(1)}) custom-call(s32[64,128]{1,0:T(8,128)S(1)} %bitcast.7), custom_call_target="tpu_custom_call" | custom-call | flops 600000000 | bytes 100000 | tf_op jit(solution)/shard_map/slots/pallas_call | solution.py:252
  30.0 1.7 %collective-permute-done.low_ref = f32[12,4,8,128]{3,2,1,0:T(8,128)S(1)} collective-permute-done((f32[12,4,8,128]{3,2,1,0:T(8,128)S(1)}, f32[12,4,8,128]{3,2,1,0:T(8,128)S(1)}, u32[]{:S(2)}, u32[]{:S(2)}) %collective-permute-start) | collective-permute-done | bytes 196640 | tf_op jit(solution)/shard_map/ppermute | solution.py:329
  31.7 1.2 %collective-permute-done.1.high_ref = f32[12,4,8,128]{3,2,1,0:T(8,128)S(1)} collective-permute-done((f32[12,4,8,128]{3,2,1,0:T(8,128)S(1)}, f32[12,4,8,128]{3,2,1,0:T(8,128)S(1)}, u32[]{:S(2)}, u32[]{:S(2)}) %collective-permute-start.1) | collective-permute-done | bytes 196640 | tf_op jit(solution)/shard_map/ppermute | solution.py:330
  32.9 4.0 %flow.1 = f32[16,64,128]{2,1,0:T(8,128)} custom-call(f32[16,4,8,128]{3,2,1,0:T(8,128)S(1)} %all_to_all.15.own_ref, f32[12,4,8,128]{3,2,1,0:T(8,128)S(1)} %collective-permute-done.low_ref, f32[12,4,8,128]{3,2,1,0:T(8,128)S(1)} %collective-permute-done.1.high_ref), custom_call_target="tpu_custom_call" | custom-call | flops 30000000 | bytes 1000000 | tf_op jit(solution)/shard_map/flow/pallas_call | solution.py:205
  36.9 4.8 %all-to-all-start.1 = ((f32[16,64,128]{2,1,0:T(8,128)}), f32[16,64,128]{2,1,0:T(8,128)S(1)}, u32[]{:S(2)}, u32[]{:S(2)}) async-start(f32[16,64,128]{2,1,0:T(8,128)} %flow.1), calls=%async_computation.1 | async-start | bytes 1048576 | tf_op jit(solution)/shard_map/all_to_all | solution.py:321
  41.7 9.8 %all-to-all-done.1.table_ref = f32[16,64,128]{2,1,0:T(8,128)S(1)} async-done(((f32[16,64,128]{2,1,0:T(8,128)}), f32[16,64,128]{2,1,0:T(8,128)S(1)}, u32[]{:S(2)}, u32[]{:S(2)}) %all-to-all-start.1) | async-done | bytes 524320 | tf_op jit(solution)/shard_map/all_to_all | solution.py:321
  51.4 3.1 %gather.1 = f32[32,16,128]{2,1,0:T(8,128)S(1)} custom-call(s32[1]{0:T(128)} %bitcast.first_ref, f32[16,64,128]{2,1,0:T(8,128)S(1)} %all-to-all-done.1.table_ref, s32[2,4,8,128]{3,2,1,0:T(8,128)S(1)} %get-tuple-element.17.owner_ref, s32[2,4,8,128]{3,2,1,0:T(8,128)S(1)} %get-tuple-element.18.rank_ref), custom_call_target="tpu_custom_call" | custom-call | flops 2200000000 | bytes 1000000 | tf_op jit(solution)/shard_map/gather/pallas_call | solution.py:309
  54.6 33.1 %all_to_all.16 = f32[32,16,128]{2,1,0:T(8,128)S(1)} all-to-all(f32[32,16,128]{2,1,0:T(8,128)S(1)} %gather.1), channel_id=1, replica_groups=mesh['xl'=2,'co'=2,'xh'=2,'z'=16,'y'=4] {'xh','z'}, dimensions={0} | all-to-all | bytes 524288 | tf_op jit(solution)/shard_map/all_to_all | solution.py:321
  87.7 0.7 copy.3
  (1 shorter events, 0.0 us)
Async XLA Ops:
  16.2 12.3 %copy-start = (s32[8192,1]{0,1:T(1,128)S(1)}, s32[8192,1]{0,1:T(1,128)}, u32[]{:S(2)}) copy-start(s32[8192,1]{0,1:T(1,128)} %param.3) | copy-start | bytes 98308
  16.2 15.5 %collective-permute-start = (f32[12,4,8,128]{3,2,1,0:T(8,128)S(1)}, f32[12,4,8,128]{3,2,1,0:T(8,128)S(1)}, u32[]{:S(2)}, u32[]{:S(2)}) collective-permute-start(f32[12,4,8,128]{3,2,1,0:T(8,128)S(1)} %get-tuple-element.20), channel_id=1, source_target_pairs={{0,4},{4,8},{8,12},{12,16},{16,20},{20,24},{24,28},{28,32},{32,36}... | collective-permute-start | bytes 589832 | tf_op jit(solution)/shard_map/ppermute | solution.py:329
  18.1 14.8 %collective-permute-start.1 = (f32[12,4,8,128]{3,2,1,0:T(8,128)S(1)}, f32[12,4,8,128]{3,2,1,0:T(8,128)S(1)}, u32[]{:S(2)}, u32[]{:S(2)}) collective-permute-start(f32[12,4,8,128]{3,2,1,0:T(8,128)S(1)} %get-tuple-element.19), channel_id=1, source_target_pairs={{4,0},{8,4},{12,8},{16,12},{20,16},{24,20},{28,24},{32,28},{36,32}... | collective-permute-start | bytes 589832 | tf_op jit(solution)/shard_map/ppermute | solution.py:330
  36.9 14.5 %all-to-all-start.1 = ((f32[16,64,128]{2,1,0:T(8,128)}), f32[16,64,128]{2,1,0:T(8,128)S(1)}, u32[]{:S(2)}, u32[]{:S(2)}) async-start(f32[16,64,128]{2,1,0:T(8,128)} %flow.1), calls=%async_computation.1 | async-start | bytes 1048576 | tf_op jit(solution)/shard_map/all_to_all | solution.py:321

commit v3 on v2

--- a/solution.py
+++ b/solution.py
@@ -38,18 +38,43 @@
 
 
 def pack_kernel(x_ref, out_ref):
-    right_lane = lanes_of((4, 128)) < 64
-    for r in range(4):
-        chunks = [x_ref[:, r, 128 * c : 128 * c + 128] for c in range(CHUNKS)]
-        for c in range(CHUNKS):
-            out_ref[c, r, 0:4, :] = chunks[c]
-            out_ref[c, r, 4:8, :] = jnp.where(right_lane, chunks[(c + 1) % CHUNKS], chunks[c - 1])
+    lane = lanes_of((8, 128))
+    rows = [[x_ref[:, r, 128 * c : 128 * c + 128] for r in range(4)] for c in range(CHUNKS)]
+    for c in range(CHUNKS):
+        right, left = rows[(c + 1) % CHUNKS], rows[c - 1]
+        for r in range(4):
+            out_ref[c, 4 * r : 4 * r + 4, :] = rows[c][r]
+        near, far = (
+            jnp.where(lane < 64, jnp.concatenate([right[r], right[r + 2]], 0), jnp.concatenate([left[r], left[r + 2]], 0))
+            for r in range(2)
+        )
+        far = jnp.where(lane < 64, pltpu.roll(far, 32, 1), pltpu.roll(far, 96, 1))
+        out_ref[c, 16:24, :] = jnp.where((lane < 32) | (lane >= 96), near, far)
+
+
+def unpacked(piece):
+    lane, sub = lanes_of((8, 128)), lax.broadcasted_iota(jnp.int32, (8, 128), 0)
+    first, second, near = piece[0:8], piece[8:16], piece[16:24]
+    far = jnp.where(lane < 64, pltpu.roll(near, 96, 1), pltpu.roll(near, 32, 1))
+
+    def joined(own, around):
+        return jnp.where(sub < 4, own, around)
+
+    def turned(x):
+        return pltpu.roll(x, 4, 0)
+
+    return (
+        joined(first, turned(near)),
+        joined(turned(first), turned(far)),
+        joined(second, near),
+        joined(turned(second), far),
+    )
 
 
 def pack(x):
     return pl.pallas_call(
         pack_kernel,
-        out_shape=pltpu.VMEM((CHUNKS, 4, 8, 128), jnp.float32),
+        out_shape=pltpu.VMEM((CHUNKS, 24, 128), jnp.float32),
         in_specs=whole(1),
         out_specs=whole(1)[0],
         cost_estimate=cost(100_000, 400_000),
@@ -112,7 +137,8 @@
     for ref, count, base in ((low_ref, 3, 0), (own_ref, 4, 12), (high_ref, 3, 28)):
         for j in range(count):
             for g in range(4):
-                fields[g, base + 4 * j : base + 4 * j + 4] = ref[4 * j + g]
+                for r, row in enumerate(unpacked(ref[4 * j + g])):
+                    fields[g, base + 4 * j + r] = row
 
     shape = (4, 8, 128)
     lane = lanes_of(shape)
@@ -329,9 +355,9 @@
     low = lax.ppermute(own[4:16], LONG_AXES, up)
     high = lax.ppermute(own[0:12], LONG_AXES, [(b, a) for a, b in up])
     owner, rank = slots(lines)
-    own, owner, rank = lax.optimization_barrier((own, owner, rank))
+    first = lax.axis_index("y").astype(jnp.int32).reshape(1)
+    own, owner, rank, first = lax.optimization_barrier((own, owner, rank, first))
     table = swap(flow(own, low, high), BLOCK_AXES)
-    first = lax.axis_index("y").astype(jnp.int32).reshape(1)
     outgoing = gather(first, table, owner, rank)
     record = swap(outgoing, LONG_AXES)
     record = record.reshape(32, 2, 8, 128).transpose(1, 0, 2, 3).reshape(512, 128)

time: 88.8 us -> 85.5 us (0.963)
  blocking collectives: 48.3 us -> 55.4 us
  waiting for transfers between devices: 12.6 us -> 7.74 us
  starting transfers between devices: 17 us -> 12.2 us
    all_to_all x1 -> x0, waiting for transfers between devices: 9.78 us -> none  [swap(): return lax.all_to_all(x, axes, split_axis=0, concat_axis=0, tiled=True)]
    all_to_all x2 -> x3, blocking collectives: 48.3 us -> 55.4 us  [swap(): return lax.all_to_all(x, axes, split_axis=0, concat_axis=0, tiled=True)]
    ppermute x1, waiting for transfers between devices: 1.67 us -> 7.73 us  [body(): low = lax.ppermute(own[4:16], LONG_AXES, up)]
    all_to_all x1 -> x0, starting transfers between devices: 4.75 us -> none  [swap(): return lax.all_to_all(x, axes, split_axis=0, concat_axis=0, tiled=True)]
    ppermute x1, waiting for transfers between devices: 1.18 us -> 0.01 us  [body(): high = lax.ppermute(own[0:12], LONG_AXES, [(b, a) for a, b in up])]
  transfers between devices with their start and end apart: 3 -> 2, of which waited for: 3 -> 1; matrix products, arithmetic and copies ran while one was open for 0% -> 0% of each run, Pallas kernels for 2% -> 2%
where the time goes in v3:
time: 85.5 us; the launch traced here: 85.2 us
  blocking collectives  55.4 us (65%)
  starting transfers between devices  12.2 us (14%)
  Pallas kernels  9.02 us (11%)
  waiting for transfers between devices  7.74 us (9%)
    all_to_all x3, blocking collectives, swap(): return lax.all_to_all(x, axes, split_axis=0, concat_axis=0, tiled=True)  55.4 us
    ppermute x1, starting transfers between devices, body(): high = lax.ppermute(own[0:12], LONG_AXES, [(b, a) for a, b in up])  10.3 us
    ppermute x1, waiting for transfers between devices, body(): low = lax.ppermute(own[4:16], LONG_AXES, up)  7.73 us
    pallas_call x1, Pallas kernels, flow(): pl.pallas_call(flow_kernel, out_shape=pltpu.VMEM((16, 64, 128), jnp.float...  3.34 us
    pallas_call x1, Pallas kernels, gather(): pl.pallas_call(gather_kernel, out_shape=jax.ShapeDtypeStruct((32, 16, 128...  3.11 us
    ppermute x1, starting transfers between devices, body(): low = lax.ppermute(own[4:16], LONG_AXES, up)  1.92 us
  transfers between devices with their start and end apart: 2, of which 1 were waited for; matrix products, arithmetic and copies ran while one was open for 0% of the time, Pallas kernels for 2%

profile of v3, /device:TPU:2, one launch (start us, length us, event | category | flops | bytes accessed | tf_op | source)
XLA Modules:
  0.0 85.2 jit_solution(560402530648385000)
XLA Ops:
  0.0 1.0 %pack.1 = f32[16,24,128]{2,1,0:T(8,128)S(1)} custom-call(f32[4,4,2048]{2,1,0:T(4,128)} %bitcast.9), custom_call_target="tpu_custom_call" | custom-call | flops 100000 | bytes 400000 | tf_op jit(solution)/shard_map/pack/pallas_call | solution.py:75
  1.0 14.2 %all_to_all.15.own_ref = f32[16,24,128]{2,1,0:T(8,128)S(1)} all-to-all(f32[16,24,128]{2,1,0:T(8,128)S(1)} %pack.1), channel_id=1, replica_groups=mesh['xl'=2,'co'=2,'xh'=2,'z'=16,'y'=4] {'y','xl','co'}, dimensions={0} | all-to-all | bytes 393216 | tf_op jit(solution)/shard_map/all_to_all | solution.py:347
  15.2 0.0 copy-start
  15.3 10.3 %collective-permute-start.1 = (f32[12,24,128]{2,1,0:T(8,128)S(1)}, f32[12,24,128]{2,1,0:T(8,128)S(1)}, u32[]{:S(2)}, u32[]{:S(2)}) collective-permute-start(f32[12,24,128]{2,1,0:T(8,128)S(1)} %get-tuple-element.21), channel_id=1, source_target_pairs={{4,0},{8,4},{12,8},{16,12},{20,16},{24,20},{28,24},{32,28},{36,32}... | collective-permute-start | bytes 442376 | tf_op jit(solution)/shard_map/ppermute | solution.py:356
  25.6 1.9 %collective-permute-start = (f32[12,24,128]{2,1,0:T(8,128)S(1)}, f32[12,24,128]{2,1,0:T(8,128)S(1)}, u32[]{:S(2)}, u32[]{:S(2)}) collective-permute-start(f32[12,24,128]{2,1,0:T(8,128)S(1)} %get-tuple-element.22), channel_id=1, source_target_pairs={{0,4},{4,8},{8,12},{12,16},{16,20},{20,24},{24,28},{28,32},{32,36}... | collective-permute-start | bytes 442376 | tf_op jit(solution)/shard_map/ppermute | solution.py:355
  27.5 0.0 copy-done
  27.6 1.5 %slots.1 = (s32[2,4,8,128]{3,2,1,0:T(8,128)S(1)}, s32[2,4,8,128]{3,2,1,0:T(8,128)S(1)}) custom-call(s32[64,128]{1,0:T(8,128)S(1)} %bitcast.7), custom_call_target="tpu_custom_call" | custom-call | flops 600000000 | bytes 100000 | tf_op jit(solution)/shard_map/slots/pallas_call | solution.py:278
  29.1 0.0 collective-permute-done.1.high_ref
  29.1 7.7 %collective-permute-done.low_ref = f32[12,24,128]{2,1,0:T(8,128)S(1)} collective-permute-done((f32[12,24,128]{2,1,0:T(8,128)S(1)}, f32[12,24,128]{2,1,0:T(8,128)S(1)}, u32[]{:S(2)}, u32[]{:S(2)}) %collective-permute-start) | collective-permute-done | bytes 147488 | tf_op jit(solution)/shard_map/ppermute | solution.py:355
  36.8 3.3 %flow.1 = f32[16,64,128]{2,1,0:T(8,128)S(1)} custom-call(f32[16,24,128]{2,1,0:T(8,128)S(1)} %all_to_all.15.own_ref, f32[12,24,128]{2,1,0:T(8,128)S(1)} %collective-permute-done.low_ref, f32[12,24,128]{2,1,0:T(8,128)S(1)} %collective-permute-done.1.high_ref), custom_call_target="tpu_custom_call" | custom-call | flops 30000000 | bytes 1000000 | tf_op jit(solution)/shard_map/flow/pallas_call | solution.py:231
  40.2 13.9 %all_to_all.16.table_ref = f32[16,64,128]{2,1,0:T(8,128)S(1)} all-to-all(f32[16,64,128]{2,1,0:T(8,128)S(1)} %flow.1), channel_id=1, replica_groups=mesh['xl'=2,'co'=2,'xh'=2,'z'=16,'y'=4] {'y','xl','co'}, dimensions={0} | all-to-all | bytes 1048576 | tf_op jit(solution)/shard_map/all_to_all | solution.py:347
  54.1 3.1 %gather.1 = f32[32,16,128]{2,1,0:T(8,128)S(1)} custom-call(s32[1]{0:T(128)} %bitcast.2.first_ref, f32[16,64,128]{2,1,0:T(8,128)S(1)} %all_to_all.16.table_ref, s32[2,4,8,128]{3,2,1,0:T(8,128)S(1)} %get-tuple-element.19.owner_ref, s32[2,4,8,128]{3,2,1,0:T(8,128)S(1)} %get-tuple-element.20.rank_ref), custom_call_target="tpu_custom_call" | custom-call | flops 2200000000 | bytes 1000000 | tf_op jit(solution)/shard_map/gather/pallas_call | solution.py:335
  57.2 27.2 %all_to_all.17 = f32[32,16,128]{2,1,0:T(8,128)S(1)} all-to-all(f32[32,16,128]{2,1,0:T(8,128)S(1)} %gather.1), channel_id=1, replica_groups=mesh['xl'=2,'co'=2,'xh'=2,'z'=16,'y'=4] {'xh','z'}, dimensions={0} | all-to-all | bytes 524288 | tf_op jit(solution)/shard_map/all_to_all | solution.py:347
  84.5 0.7 copy.3
  (1 shorter events, 0.0 us)
Async XLA Ops:
  15.2 12.3 %copy-start = (s32[8192,1]{0,1:T(1,128)S(1)}, s32[8192,1]{0,1:T(1,128)}, u32[]{:S(2)}) copy-start(s32[8192,1]{0,1:T(1,128)} %param.3) | copy-start | bytes 98308
  15.3 13.8 %collective-permute-start.1 = (f32[12,24,128]{2,1,0:T(8,128)S(1)}, f32[12,24,128]{2,1,0:T(8,128)S(1)}, u32[]{:S(2)}, u32[]{:S(2)}) collective-permute-start(f32[12,24,128]{2,1,0:T(8,128)S(1)} %get-tuple-element.21), channel_id=1, source_target_pairs={{4,0},{8,4},{12,8},{16,12},{20,16},{24,20},{28,24},{32,28},{36,32}... | collective-permute-start | bytes 442376 | tf_op jit(solution)/shard_map/ppermute | solution.py:356
  25.6 11.2 %collective-permute-start = (f32[12,24,128]{2,1,0:T(8,128)S(1)}, f32[12,24,128]{2,1,0:T(8,128)S(1)}, u32[]{:S(2)}, u32[]{:S(2)}) collective-permute-start(f32[12,24,128]{2,1,0:T(8,128)S(1)} %get-tuple-element.22), channel_id=1, source_target_pairs={{0,4},{4,8},{8,12},{12,16},{16,20},{20,24},{24,28},{28,32},{32,36}... | collective-permute-start | bytes 442376 | tf_op jit(solution)/shard_map/ppermute | solution.py:355

commit v4 on v3

--- a/solution.py
+++ b/solution.py
@@ -8,6 +8,7 @@
 
 BLOCK_AXES = ("y", "xl", "co")
 LONG_AXES = ("xh", "z")
+LAST_AXES = ("z", "xh")
 
 time_step = 0.2
 viscosity = 0.05
@@ -245,7 +246,7 @@
     )(own, low, high)
 
 
-def slots_kernel(owner_ref, owner_out, rank_out, rank_rows):
+def slots_kernel(first_ref, owner_ref, lower_out, place_out, rank_rows):
     bf16, f32 = jnp.bfloat16, jnp.float32
     row = lax.broadcasted_iota(jnp.int32, (128, 128), 0)
     lane = lanes_of((128, 128))
@@ -258,89 +259,81 @@
         ranks = jnp.where(mine, base + counts[:, 0:128], 0.0)
         rank_rows[b : b + 1, :] = jnp.sum(ranks, axis=0, keepdims=True)
         base = base + counts[:, 128:256]
-    owners = owner_ref[...].astype(f32).astype(bf16)
-    ranks = rank_rows[...].astype(bf16)
+    owners, ranks = owner_ref[...].astype(f32), rank_rows[...]
     for part in range(2):
-        even = jnp.where(lane == 2 * (row - 64 * part), 1.0, 0.0).astype(bf16)
-        odd = jnp.where(lane == 2 * (row - 64 * part) + 1, 1.0, 0.0).astype(bf16)
-        for values, out in ((owners, owner_out), (ranks, rank_out)):
-            from_even = jnp.dot(values, even, preferred_element_type=f32)
-            from_odd = jnp.dot(values, odd, preferred_element_type=f32)
-            for z in range(PLANES):
-                plane = (0, 2, 1, 3)[z]
-                low = from_even[16 * plane : 16 * plane + 8]
-                high = from_odd[16 * plane + 8 : 16 * plane + 16]
-                out[part, z, :, :] = (low + high).astype(jnp.int32)
-
-
-def slots(owner_rows):
-    shape = jax.ShapeDtypeStruct((2, PLANES, 8, 128), jnp.int32)
+        even = jnp.where(lane == 2 * (row - 64 * part), 1.0, 0.0)
+        odd = jnp.where(lane == 2 * (row - 64 * part) + 1, 1.0, 0.0)
+        for z in range(PLANES):
+            plane = (0, 2, 1, 3)[z]
+            low, high = slice(16 * plane, 16 * plane + 8), slice(16 * plane + 8, 16 * plane + 16)
+            owner, rank = (
+                jnp.dot(values[low], even, preferred_element_type=f32)
+                + jnp.dot(values[high], odd, preferred_element_type=f32)
+                for values in (owners, ranks)
+            )
+            owner = owner.astype(jnp.int32)
+            pencil = owner // 4
+            lower = jnp.where(owner % 4 == first_ref[0], pencil % 16, -1)
+            lower_out[part, z, :, :] = lower.astype(f32)
+            place_out[part, z, :, :] = (128 * (pencil // 16)).astype(f32) + rank
+
+
+def slots(first, owner_rows):
+    shape = jax.ShapeDtypeStruct((2, PLANES, 8, 128), jnp.float32)
     return pl.pallas_call(
         slots_kernel,
         out_shape=(shape, shape),
-        in_specs=whole(1),
+        in_specs=[pl.BlockSpec(memory_space=pltpu.SMEM)] + whole(1),
         out_specs=tuple(whole(2)),
         scratch_shapes=[pltpu.VMEM((64, 128), jnp.float32)],
         compiler_params=pltpu.CompilerParams(vmem_limit_bytes=VMEM_LIMIT),
         cost_estimate=cost(600_000_000, 100_000),
         name="slots",
-    )(owner_rows)
-
-
-def gather_kernel(first_ref, table_ref, owner_ref, rank_ref, out_ref):
+    )(first, owner_rows)
+
+
+def gather_kernel(table_ref, lower_ref, place_ref, out_ref):
     bf16, f32 = jnp.bfloat16, jnp.float32
-    first = first_ref[0]
     slot = lax.broadcasted_iota(jnp.int32, (256, 128), 0).astype(f32).astype(bf16)
-    nothing = jnp.zeros((16, 128), bf16)
-
-    def spread(row, rows):
-        return jnp.broadcast_to(row, (rows, 128)).astype(f32).astype(bf16)
-
-    def chunk(c, carry):
-        moved = None
-        for z in range(PLANES):
-            values = table_ref[c, pl.ds(z, 16, stride=4), :]
-            high = values.astype(bf16)
-            low = (values - high.astype(f32)).astype(bf16)
-            owner = owner_ref[c % 2, z, pl.ds(c // 2, 1), :]
-            rank = rank_ref[c % 2, z, pl.ds(c // 2, 1), :]
-            mine = owner % 4 == first
-            pencil = owner // 4
-            lower = spread(jnp.where(mine, pencil % 16, -1), 16)
-            at = spread(jnp.where(mine, 128 * (pencil // 16) + rank, -1), 16)
-            left = []
-            for t in range(16):
-                hit = lower == jnp.asarray(t, bf16)
-                left.append(jnp.concatenate([jnp.where(hit, high, nothing), jnp.where(hit, low, nothing)], 1))
-            ones = jnp.ones((16, 128), bf16)
-            right = [jnp.where(at == slot[16 * k : 16 * k + 16], ones, nothing) for k in range(16)]
-            right = jnp.concatenate(right, 0)
+    nothing, ones = jnp.zeros((16, 128), bf16), jnp.ones((16, 128), bf16)
+    total = None
+    for c in range(CHUNKS):
+        for pair in range(2):
+            left, right = [], []
+            for z in (2 * pair, 2 * pair + 1):
+                values = table_ref[c, pl.ds(z, 16, stride=4), :]
+                high = values.astype(bf16)
+                low = (values - high.astype(f32)).astype(bf16)
+                lower, place = (
+                    jnp.broadcast_to(ref[c % 2, z, c // 2 : c // 2 + 1, :], (16, 128)).astype(bf16)
+                    for ref in (lower_ref, place_ref)
+                )
+                hits = [lower == jnp.asarray(t, bf16) for t in range(16)]
+                left.append(jnp.concatenate([jnp.where(hit, x, nothing) for x in (high, low) for hit in hits], 0))
+                at = [jnp.where(place == slot[16 * k : 16 * k + 16], ones, nothing) for k in range(16)]
+                right.append(jnp.concatenate(at, 0))
             part = lax.dot_general(
-                jnp.concatenate(left, 0),
-                jnp.concatenate([right, right], 1),
+                jnp.concatenate(left, 1),
+                jnp.concatenate(right, 1),
                 (((1,), (1,)), ((), ())),
                 preferred_element_type=f32,
             )
-            moved = part if moved is None else moved + part
-        for upper in range(2):
-            part = moved[:, 128 * upper : 128 * upper + 128].reshape(16, 16, 128)
-            rows = slice(16 * upper, 16 * upper + 16)
-            out_ref[rows] = jnp.where(c == 0, part, out_ref[rows] + part)
-        return carry
-
-    lax.fori_loop(0, CHUNKS, chunk, 0, unroll=4)
-
-
-def gather(first, table, owner, rank):
+            total = part if total is None else total + part
+    total = total[0:256] + total[256:512]
+    for upper in range(2):
+        out_ref[:, upper] = total[:, 128 * upper : 128 * upper + 128].reshape(16, 16, 128)
+
+
+def gather(table, lower, place):
     return pl.pallas_call(
         gather_kernel,
-        out_shape=jax.ShapeDtypeStruct((32, 16, 128), jnp.float32),
-        in_specs=[pl.BlockSpec(memory_space=pltpu.SMEM)] + whole(3),
+        out_shape=jax.ShapeDtypeStruct((16, 2, 16, 128), jnp.float32),
+        in_specs=whole(3),
         out_specs=whole(1)[0],
         compiler_params=pltpu.CompilerParams(vmem_limit_bytes=VMEM_LIMIT),
         cost_estimate=cost(2_200_000_000, 1_000_000),
         name="gather",
-    )(first, table, owner, rank)
+    )(table, lower, place)
 
 
 def swap(x, axes):
@@ -354,13 +347,12 @@
     own, lines = lax.optimization_barrier((own, line_owner.reshape(64, 128)))
     low = lax.ppermute(own[4:16], LONG_AXES, up)
     high = lax.ppermute(own[0:12], LONG_AXES, [(b, a) for a, b in up])
-    owner, rank = slots(lines)
     first = lax.axis_index("y").astype(jnp.int32).reshape(1)
-    own, owner, rank, first = lax.optimization_barrier((own, owner, rank, first))
+    own, lower, place = lax.optimization_barrier((own, *slots(first, lines)))
     table = swap(flow(own, low, high), BLOCK_AXES)
-    outgoing = gather(first, table, owner, rank)
-    record = swap(outgoing, LONG_AXES)
-    record = record.reshape(32, 2, 8, 128).transpose(1, 0, 2, 3).reshape(512, 128)
+    outgoing = gather(table, lower, place).reshape(32, 16, 128)
+    record = swap(outgoing, LAST_AXES)
+    record = record.reshape(16, 2, 2, 8, 128).transpose(2, 1, 0, 3, 4).reshape(512, 128)
     return record[None, None]
 
 

time: 85.5 us -> 83.8 us (0.980)
  the two profiles are of different devices: /device:TPU:2 before, /device:TPU:6 now
where the time goes in v4:
time: 83.8 us; the launch traced here: 83.4 us
  blocking collectives  52.5 us (63%)
  starting transfers between devices  14.2 us (17%)
  Pallas kernels  8.39 us (10%)
  waiting for transfers between devices  7.62 us (9%)
    all_to_all x3, blocking collectives, swap(): return lax.all_to_all(x, axes, split_axis=0, concat_axis=0, tiled=True)  52.5 us
    ppermute x1, starting transfers between devices, body(): high = lax.ppermute(own[0:12], LONG_AXES, [(b, a) for a, b in up])  12.2 us
    ppermute x1, waiting for transfers between devices, body(): low = lax.ppermute(own[4:16], LONG_AXES, up)  7.62 us
    pallas_call x1, Pallas kernels, flow(): pl.pallas_call(flow_kernel, out_shape=pltpu.VMEM((16, 64, 128), jnp.float...  3.34 us
    pallas_call x1, Pallas kernels, gather(): pl.pallas_call(gather_kernel, out_shape=jax.ShapeDtypeStruct((16, 2, 16,...  2.37 us
    ppermute x1, starting transfers between devices, body(): low = lax.ppermute(own[4:16], LONG_AXES, up)  1.92 us
  transfers between devices with their start and end apart: 2, of which 1 were waited for; matrix products, arithmetic and copies ran while one was open for 0% of the time, Pallas kernels for 2%

profile of v4, /device:TPU:6, one launch (start us, length us, event | category | flops | bytes accessed | tf_op | source)
XLA Modules:
  0.0 83.4 jit_solution(3243645982487175439)
XLA Ops:
  0.0 1.0 %pack.1 = f32[16,24,128]{2,1,0:T(8,128)S(1)} custom-call(f32[4,4,2048]{2,1,0:T(4,128)} %bitcast.11), custom_call_target="tpu_custom_call" | custom-call | flops 100000 | bytes 400000 | tf_op jit(solution)/shard_map/pack/pallas_call | solution.py:76
  1.0 11.6 %all_to_all.15.own_ref = f32[16,24,128]{2,1,0:T(8,128)S(1)} all-to-all(f32[16,24,128]{2,1,0:T(8,128)S(1)} %pack.1), channel_id=1, replica_groups=mesh['xl'=2,'co'=2,'xh'=2,'z'=16,'y'=4] {'y','xl','co'}, dimensions={0} | all-to-all | bytes 393216 | tf_op jit(solution)/shard_map/all_to_all | solution.py:340
  12.6 0.0 copy-start
  12.6 12.2 %collective-permute-start.1 = (f32[12,24,128]{2,1,0:T(8,128)S(1)}, f32[12,24,128]{2,1,0:T(8,128)S(1)}, u32[]{:S(2)}, u32[]{:S(2)}) collective-permute-start(f32[12,24,128]{2,1,0:T(8,128)S(1)} %get-tuple-element.19), channel_id=1, source_target_pairs={{4,0},{8,4},{12,8},{16,12},{20,16},{24,20},{28,24},{32,28},{36,32}... | collective-permute-start | bytes 442376 | tf_op jit(solution)/shard_map/ppermute | solution.py:349
  24.9 1.9 %collective-permute-start = (f32[12,24,128]{2,1,0:T(8,128)S(1)}, f32[12,24,128]{2,1,0:T(8,128)S(1)}, u32[]{:S(2)}, u32[]{:S(2)}) collective-permute-start(f32[12,24,128]{2,1,0:T(8,128)S(1)} %get-tuple-element.20), channel_id=1, source_target_pairs={{0,4},{4,8},{8,12},{12,16},{16,20},{20,24},{24,28},{28,32},{32,36}... | collective-permute-start | bytes 442376 | tf_op jit(solution)/shard_map/ppermute | solution.py:348
  26.8 0.0 copy-done
  26.8 1.7 %slots.1 = (f32[2,4,8,128]{3,2,1,0:T(8,128)S(1)}, f32[2,4,8,128]{3,2,1,0:T(8,128)S(1)}) custom-call(s32[1]{0:T(128)} %bitcast.2.first_ref, s32[64,128]{1,0:T(8,128)S(1)} %bitcast.9), custom_call_target="tpu_custom_call" | custom-call | flops 600000000 | bytes 100000 | tf_op jit(solution)/shard_map/slots/pallas_call | solution.py:283
  28.5 0.0 collective-permute-done.1.high_ref
  28.5 7.6 %collective-permute-done.low_ref = f32[12,24,128]{2,1,0:T(8,128)S(1)} collective-permute-done((f32[12,24,128]{2,1,0:T(8,128)S(1)}, f32[12,24,128]{2,1,0:T(8,128)S(1)}, u32[]{:S(2)}, u32[]{:S(2)}) %collective-permute-start) | collective-permute-done | bytes 147488 | tf_op jit(solution)/shard_map/ppermute | solution.py:348
  36.1 3.3 %flow.1 = f32[16,64,128]{2,1,0:T(8,128)S(1)} custom-call(f32[16,24,128]{2,1,0:T(8,128)S(1)} %all_to_all.15.own_ref, f32[12,24,128]{2,1,0:T(8,128)S(1)} %collective-permute-done.low_ref, f32[12,24,128]{2,1,0:T(8,128)S(1)} %collective-permute-done.1.high_ref), custom_call_target="tpu_custom_call" | custom-call | flops 30000000 | bytes 1000000 | tf_op jit(solution)/shard_map/flow/pallas_call | solution.py:232
  39.5 13.5 %all_to_all.16.table_ref = f32[16,64,128]{2,1,0:T(8,128)S(1)} all-to-all(f32[16,64,128]{2,1,0:T(8,128)S(1)} %flow.1), channel_id=1, replica_groups=mesh['xl'=2,'co'=2,'xh'=2,'z'=16,'y'=4] {'y','xl','co'}, dimensions={0} | all-to-all | bytes 1048576 | tf_op jit(solution)/shard_map/all_to_all | solution.py:340
  52.9 2.4 %gather.1 = f32[16,2,16,128]{3,2,1,0:T(8,128)S(1)} custom-call(f32[16,64,128]{2,1,0:T(8,128)S(1)} %all_to_all.16.table_ref, f32[2,4,8,128]{3,2,1,0:T(8,128)S(1)} %get-tuple-element.17.lower_ref, f32[2,4,8,128]{3,2,1,0:T(8,128)S(1)} %get-tuple-element.18.place_ref), custom_call_target="tpu_custom_call" | custom-call | flops 2200000000 | bytes 1000000 | tf_op jit(solution)/shard_map/gather/pallas_call | solution.py:328
  55.3 27.4 %all_to_all.17 = f32[32,16,128]{2,1,0:T(8,128)S(1)} all-to-all(f32[32,16,128]{2,1,0:T(8,128)S(1)} %bitcast.8), channel_id=1, replica_groups=mesh['xl'=2,'co'=2,'xh'=2,'z'=16,'y'=4] {'z','xh'}, dimensions={0} | all-to-all | bytes 524288 | tf_op jit(solution)/shard_map/all_to_all | solution.py:340
  82.7 0.7 copy.3
  (1 shorter events, 0.0 us)
Async XLA Ops:
  12.6 14.2 %copy-start = (s32[8192,1]{0,1:T(1,128)S(1)}, s32[8192,1]{0,1:T(1,128)}, u32[]{:S(2)}) copy-start(s32[8192,1]{0,1:T(1,128)} %param.3) | copy-start | bytes 98308
  12.6 15.9 %collective-permute-start.1 = (f32[12,24,128]{2,1,0:T(8,128)S(1)}, f32[12,24,128]{2,1,0:T(8,128)S(1)}, u32[]{:S(2)}, u32[]{:S(2)}) collective-permute-start(f32[12,24,128]{2,1,0:T(8,128)S(1)} %get-tuple-element.19), channel_id=1, source_target_pairs={{4,0},{8,4},{12,8},{16,12},{20,16},{24,20},{28,24},{32,28},{36,32}... | collective-permute-start | bytes 442376 | tf_op jit(solution)/shard_map/ppermute | solution.py:349
  24.9 11.2 %collective-permute-start = (f32[12,24,128]{2,1,0:T(8,128)S(1)}, f32[12,24,128]{2,1,0:T(8,128)S(1)}, u32[]{:S(2)}, u32[]{:S(2)}) collective-permute-start(f32[12,24,128]{2,1,0:T(8,128)S(1)} %get-tuple-element.20), channel_id=1, source_target_pairs={{0,4},{4,8},{8,12},{12,16},{16,20},{20,24},{24,28},{28,32},{32,36}... | collective-permute-start | bytes 442376 | tf_op jit(solution)/shard_map/ppermute | solution.py:348

commit v5 on v4

--- a/solution.py
+++ b/solution.py
@@ -1,5 +1,6 @@
 import jax
 import jax.numpy as jnp
+import numpy as np
 from jax import lax
 from jax.experimental import pallas as pl
 from jax.experimental.pallas import tpu as pltpu
@@ -91,11 +92,36 @@
     return weights
 
 
-def column_shifts(here, lane, reach):
-    other = pltpu.roll(here, 4, 1)
-    right = [pltpu.roll(jnp.where(lane < k, other, here), 128 - k, 2) for k in range(1, reach + 1)]
-    left = [pltpu.roll(jnp.where(lane >= 128 - k, other, here), k, 2) for k in range(1, reach + 1)]
-    return right, left
+def column_weights():
+    apart = (np.arange(256)[:, None] - np.arange(128)[None, :]) % 256
+    first, second = np.zeros((256, 128)), np.zeros((256, 128))
+    taps = [np.resize(pair, 128) for pair in filter_taps(None)]
+    lift = taps[0] * (apart == 0)
+    for k in range(1, 5):
+        lift += taps[k] * ((apart == k) | (apart == 256 - k))
+        first += first_coeffs[k - 1] * ((apart == k) * 1.0 - (apart == 256 - k))
+        second += second_coeffs[k - 1] * ((apart == k) * 1.0 + (apart == 256 - k))
+    weights = np.concatenate([first, second, lift], 1)
+    high = weights.astype(jnp.bfloat16)
+    low = (weights - high.astype(np.float64)).astype(jnp.bfloat16)
+    return np.concatenate([high, high, low], 0)
+
+
+def weighted_lanes(rows, others, weights):
+    both = jnp.concatenate([rows, others], 1)
+    high = both.astype(jnp.bfloat16)
+    low = (both - high.astype(jnp.float32)).astype(jnp.bfloat16)
+    return jnp.dot(jnp.concatenate([high, low, high], 1), weights, preferred_element_type=jnp.float32)
+
+
+def column_sums(values, weights_ref):
+    rows = jnp.concatenate([v.reshape(32, 128) for v in values], 0)
+    others = jnp.concatenate([pltpu.roll(v, 4, 1).reshape(32, 128) for v in values], 0)
+    sums = weighted_lanes(rows, others, weights_ref[:, 0:256])
+    return [
+        tuple(sums[32 * n : 32 * n + 32, 128 * d : 128 * d + 128].reshape(4, 8, 128) for d in range(2))
+        for n in range(len(values))
+    ]
 
 
 def plane_shifts(here, plane):
@@ -115,71 +141,69 @@
     return total
 
 
-def derivatives(load, low, lane, plane, second=True):
+def derivatives(load, low, along_y, plane, second=True):
     here = load(low)
-    right, left = column_shifts(here, lane, 4)
+    d_y, lap_y = along_y
     up, down = ([load(low + s * k) for k in range(1, 5)] for s in (1, -1))
     over, under = plane_shifts(here, plane)
     _, forward, _, behind = folded(first_coeffs, -1.0)
     assert forward == -behind
     d_x = weighted(first_coeffs, [a - b for a, b in zip(up, down)])
-    d_y = weighted(first_coeffs, [a - b for a, b in zip(right, left)])
     d_z = forward * (over - under)
     if not second:
         return d_x, d_y, d_z
     centre, near, far, _ = folded(second_coeffs, 1.0)
-    lap = weighted(second_coeffs, [(a + b) + (c + d) for a, b, c, d in zip(up, down, right, left)])
+    lap = weighted(second_coeffs, [a + b for a, b in zip(up, down)]) + lap_y
     lap = lap + (3.0 * second_center + centre) * here
     lap = lap + (near * (over + under) + far * plane_opposite(here, plane))
     return d_x, d_y, d_z, lap
 
 
-def flow_kernel(own_ref, low_ref, high_ref, out_ref, fields, middle, slopes, lifted):
+def flow_kernel(weights_ref, own_ref, low_ref, high_ref, out_ref, fields, middle, slopes, lifted):
     for ref, count, base in ((low_ref, 3, 0), (own_ref, 4, 12), (high_ref, 3, 28)):
         for j in range(count):
             for g in range(4):
                 for r, row in enumerate(unpacked(ref[4 * j + g])):
                     fields[g, base + 4 * j + r] = row
 
-    shape = (4, 8, 128)
-    lane = lanes_of(shape)
-    plane = lax.broadcasted_iota(jnp.int32, shape, 1) % 4
+    plane = lax.broadcasted_iota(jnp.int32, (4, 8, 128), 1) % 4
 
     def loader(ref, g):
         return lambda low: ref[g, pl.ds(low, 4)]
 
     def first(i, carry):
         low = 4 + 4 * i
-        grads = derivatives(loader(fields, 3), low, lane, plane, second=False)
+        along_y = column_sums([fields[f, pl.ds(low, 4)] for f in range(4)], weights_ref)
+        grads = derivatives(loader(fields, 3), low, along_y[3], plane, second=False)
         u, v, w = (fields[f, pl.ds(low, 4)] for f in range(3))
         for g in range(3):
-            d_x, d_y, d_z, lap = derivatives(loader(fields, g), low, lane, plane)
+            d_x, d_y, d_z, lap = derivatives(loader(fields, g), low, along_y[g], plane)
             slopes[g, pl.ds(4 * i, 4)] = grads[g]
             tend = viscosity * lap - (u * d_x + v * d_y + w * d_z) - grads[g]
             middle[g, pl.ds(4 * i, 4)] = (u, v, w)[g] + time_step * tend
         return carry
 
-    lax.fori_loop(0, 8, first, 0)
+    lax.fori_loop(0, 8, first, 0, unroll=4)
 
     def second(i, carry):
         low = 4 + 4 * i
         u, v, w = (middle[f, pl.ds(low, 4)] for f in range(3))
+        along_y = column_sums([u, v, w], weights_ref)
         for g in range(3):
-            d_x, d_y, d_z, lap = derivatives(loader(middle, g), low, lane, plane)
+            d_x, d_y, d_z, lap = derivatives(loader(middle, g), low, along_y[g], plane)
             tend = viscosity * lap - (u * d_x + v * d_y + w * d_z) - slopes[g, pl.ds(low, 4)]
             s = 0.5 * ((fields[g, pl.ds(low + 4, 4)] + (u, v, w)[g]) + time_step * tend)
             lifted[g, pl.ds(4 * i, 4)] = s
         return carry
 
-    lax.fori_loop(0, 6, second, 0)
-
-    lane, sub = lanes_of((8, 128)), lax.broadcasted_iota(jnp.int32, (8, 128), 0)
-    odd_y, odd_z, first_row = lane % 2 == 1, sub % 2 == 1, sub < 4
+    lax.fori_loop(0, 6, second, 0, unroll=3)
+
+    sub = lax.broadcasted_iota(jnp.int32, (8, 128), 0)
+    odd_z, first_row = sub % 2 == 1, sub < 4
 
     def chosen(odd, pair):
         return jnp.where(odd, jnp.float32(pair[1]), jnp.float32(pair[0]))
 
-    taps = [chosen(odd_y, pair) for pair in filter_taps(None)]
     same, opposite = (chosen(odd_z, pair) for pair in filter_taps(PLANES))
     energy = [None] * 8
     for g in range(3):
@@ -189,15 +213,12 @@
         even = [None] + [even[i] + lift_beta * (odd[i] + odd[i - 1]) for i in range(1, 11)]
         odd = [None] + [odd[i] + lift_gamma * (even[i] + even[i + 1]) for i in range(1, 10)]
         even = [None, None] + [even[i] + lift_delta * (odd[i] + odd[i - 1]) for i in range(2, 10)]
+        pairs = [(even, odd)[pair // 4][2 + 2 * (pair % 4) : 4 + 2 * (pair % 4)] for pair in range(8)]
+        here = jnp.concatenate([jnp.where(first_row, a, pltpu.roll(b, 4, 0)) for a, b in pairs], 0)
+        around = jnp.concatenate([jnp.where(first_row, pltpu.roll(a, 4, 0), b) for a, b in pairs], 0)
+        along_y = weighted_lanes(here, around, weights_ref[:, 256:384])
         for pair in range(8):
-            a, b = (even, odd)[pair // 4][2 + 2 * (pair % 4) : 4 + 2 * (pair % 4)]
-            here = jnp.where(first_row, a, pltpu.roll(b, 4, 0))
-            around = jnp.where(first_row, pltpu.roll(a, 4, 0), b)
-            rows = taps[0] * here
-            for k in range(1, 5):
-                right = pltpu.roll(jnp.where(lane < k, around, here), 128 - k, 1)
-                left = pltpu.roll(jnp.where(lane >= 128 - k, around, here), k, 1)
-                rows = rows + taps[k] * (right + left)
+            rows = along_y[8 * pair : 8 * pair + 8]
             both = rows + jnp.where(sub % 4 < 2, pltpu.roll(rows, 6, 0), pltpu.roll(rows, 2, 0))
             others = jnp.where(odd_z, pltpu.roll(both, 1, 0), pltpu.roll(both, 7, 0))
             rows = rows + (same * both + opposite * others)
@@ -232,7 +253,7 @@
     return pl.pallas_call(
         flow_kernel,
         out_shape=pltpu.VMEM((16, 64, 128), jnp.float32),
-        in_specs=whole(3),
+        in_specs=whole(4),
         out_specs=whole(1)[0],
         scratch_shapes=[
             pltpu.VMEM((4, 40, 8, 128), jnp.float32),
@@ -243,7 +264,7 @@
         compiler_params=pltpu.CompilerParams(vmem_limit_bytes=VMEM_LIMIT),
         cost_estimate=cost(30_000_000, 1_000_000),
         name="flow",
-    )(own, low, high)
+    )(jnp.asarray(column_weights()), own, low, high)
 
 
 def slots_kernel(first_ref, owner_ref, lower_out, place_out, rank_rows):

time: 83.8 us -> 82.8 us (0.988)
  Pallas kernels: 8.39 us -> 7.48 us
    pallas_call x1, Pallas kernels: 3.34 us -> 2.42 us  [flow(): pl.pallas_call(flow_kernel, out_shape=pltpu.VMEM((16, 64, 128), jnp.float...]
where the time goes in v5:
time: 82.8 us; the launch traced here: 82.5 us
  blocking collectives  52.4 us (63%)
  starting transfers between devices  14.2 us (17%)
  waiting for transfers between devices  7.62 us (9%)
  Pallas kernels  7.48 us (9%)
    all_to_all x3, blocking collectives, swap(): return lax.all_to_all(x, axes, split_axis=0, concat_axis=0, tiled=True)  52.4 us
    ppermute x1, starting transfers between devices, body(): high = lax.ppermute(own[0:12], LONG_AXES, [(b, a) for a, b in up])  12.2 us
    ppermute x1, waiting for transfers between devices, body(): low = lax.ppermute(own[4:16], LONG_AXES, up)  7.61 us
    pallas_call x1, Pallas kernels, flow(): pl.pallas_call(flow_kernel, out_shape=pltpu.VMEM((16, 64, 128), jnp.float...  2.42 us
    pallas_call x1, Pallas kernels, gather(): pl.pallas_call(gather_kernel, out_shape=jax.ShapeDtypeStruct((16, 2, 16,...  2.37 us
    ppermute x1, starting transfers between devices, body(): low = lax.ppermute(own[4:16], LONG_AXES, up)  1.92 us
  transfers between devices with their start and end apart: 2, of which 1 were waited for; matrix products, arithmetic and copies ran while one was open for 0% of the time, Pallas kernels for 2%

profile of v5, /device:TPU:6, one launch (start us, length us, event | category | flops | bytes accessed | tf_op | source)
XLA Modules:
  0.0 82.5 jit_solution(1244616801959601644)
XLA Ops:
  0.0 1.0 %pack.1 = f32[16,24,128]{2,1,0:T(8,128)S(1)} custom-call(f32[4,4,2048]{2,1,0:T(4,128)} %bitcast.11), custom_call_target="tpu_custom_call" | custom-call | flops 100000 | bytes 400000 | tf_op jit(solution)/shard_map/pack/pallas_call | solution.py:77
  1.0 11.6 %all_to_all.15.own_ref = f32[16,24,128]{2,1,0:T(8,128)S(1)} all-to-all(f32[16,24,128]{2,1,0:T(8,128)S(1)} %pack.1), channel_id=1, replica_groups=mesh['xl'=2,'co'=2,'xh'=2,'z'=16,'y'=4] {'y','xl','co'}, dimensions={0} | all-to-all | bytes 393216 | tf_op jit(solution)/shard_map/all_to_all | solution.py:361
  12.6 0.0 copy-start.1
  12.6 12.2 %collective-permute-start.1 = (f32[12,24,128]{2,1,0:T(8,128)S(1)}, f32[12,24,128]{2,1,0:T(8,128)S(1)}, u32[]{:S(2)}, u32[]{:S(2)}) collective-permute-start(f32[12,24,128]{2,1,0:T(8,128)S(1)} %get-tuple-element.19), channel_id=1, source_target_pairs={{4,0},{8,4},{12,8},{16,12},{20,16},{24,20},{28,24},{32,28},{36,32}... | collective-permute-start | bytes 442376 | tf_op jit(solution)/shard_map/ppermute | solution.py:370
  24.9 1.9 %collective-permute-start = (f32[12,24,128]{2,1,0:T(8,128)S(1)}, f32[12,24,128]{2,1,0:T(8,128)S(1)}, u32[]{:S(2)}, u32[]{:S(2)}) collective-permute-start(f32[12,24,128]{2,1,0:T(8,128)S(1)} %get-tuple-element.20), channel_id=1, source_target_pairs={{0,4},{4,8},{8,12},{12,16},{16,20},{20,24},{24,28},{28,32},{32,36}... | collective-permute-start | bytes 442376 | tf_op jit(solution)/shard_map/ppermute | solution.py:369
  26.8 0.0 copy-done.1
  26.8 0.0 copy-start
  26.8 1.7 %slots.1 = (f32[2,4,8,128]{3,2,1,0:T(8,128)S(1)}, f32[2,4,8,128]{3,2,1,0:T(8,128)S(1)}) custom-call(s32[1]{0:T(128)} %bitcast.2.first_ref, s32[64,128]{1,0:T(8,128)S(1)} %bitcast.9), custom_call_target="tpu_custom_call" | custom-call | flops 600000000 | bytes 100000 | tf_op jit(solution)/shard_map/slots/pallas_call | solution.py:304
  28.5 0.0 collective-permute-done.1.high_ref
  28.5 7.6 %collective-permute-done.low_ref = f32[12,24,128]{2,1,0:T(8,128)S(1)} collective-permute-done((f32[12,24,128]{2,1,0:T(8,128)S(1)}, f32[12,24,128]{2,1,0:T(8,128)S(1)}, u32[]{:S(2)}, u32[]{:S(2)}) %collective-permute-start) | collective-permute-done | bytes 147488 | tf_op jit(solution)/shard_map/ppermute | solution.py:369
  36.1 0.0 copy-done
  36.1 2.4 %flow.1 = f32[16,64,128]{2,1,0:T(8,128)S(1)} custom-call(bf16[768,384]{1,0:T(8,128)(2,1)S(1)} %copy-done, f32[16,24,128]{2,1,0:T(8,128)S(1)} %all_to_all.15.own_ref, f32[12,24,128]{2,1,0:T(8,128)S(1)} %collective-permute-done.low_ref, f32[12,24,128]{2,1,0:T(8,128)S(1)} %collective-permute-done.1.high_ref), custom_call_target="tpu_custom_call" | custom-call | flops 30000000 | bytes 1000000 | tf_op jit(solution)/shard_map/flow/pallas_call | solution.py:253
  38.6 13.5 %all_to_all.16.table_ref = f32[16,64,128]{2,1,0:T(8,128)S(1)} all-to-all(f32[16,64,128]{2,1,0:T(8,128)S(1)} %flow.1), channel_id=1, replica_groups=mesh['xl'=2,'co'=2,'xh'=2,'z'=16,'y'=4] {'y','xl','co'}, dimensions={0} | all-to-all | bytes 1048576 | tf_op jit(solution)/shard_map/all_to_all | solution.py:361
  52.0 2.4 %gather.1 = f32[16,2,16,128]{3,2,1,0:T(8,128)S(1)} custom-call(f32[16,64,128]{2,1,0:T(8,128)S(1)} %all_to_all.16.table_ref, f32[2,4,8,128]{3,2,1,0:T(8,128)S(1)} %get-tuple-element.17.lower_ref, f32[2,4,8,128]{3,2,1,0:T(8,128)S(1)} %get-tuple-element.18.place_ref), custom_call_target="tpu_custom_call" | custom-call | flops 2200000000 | bytes 1000000 | tf_op jit(solution)/shard_map/gather/pallas_call | solution.py:349
  54.4 27.4 %all_to_all.17 = f32[32,16,128]{2,1,0:T(8,128)S(1)} all-to-all(f32[32,16,128]{2,1,0:T(8,128)S(1)} %bitcast.8), channel_id=1, replica_groups=mesh['xl'=2,'co'=2,'xh'=2,'z'=16,'y'=4] {'z','xh'}, dimensions={0} | all-to-all | bytes 524288 | tf_op jit(solution)/shard_map/all_to_all | solution.py:361
  81.8 0.7 copy.4
  (1 shorter events, 0.0 us)
Async XLA Ops:
  12.6 14.2 %copy-start.1 = (s32[8192,1]{0,1:T(1,128)S(1)}, s32[8192,1]{0,1:T(1,128)}, u32[]{:S(2)}) copy-start(s32[8192,1]{0,1:T(1,128)} %param.4) | copy-start | bytes 98308
  12.6 15.9 %collective-permute-start.1 = (f32[12,24,128]{2,1,0:T(8,128)S(1)}, f32[12,24,128]{2,1,0:T(8,128)S(1)}, u32[]{:S(2)}, u32[]{:S(2)}) collective-permute-start(f32[12,24,128]{2,1,0:T(8,128)S(1)} %get-tuple-element.19), channel_id=1, source_target_pairs={{4,0},{8,4},{12,8},{16,12},{20,16},{24,20},{28,24},{32,28},{36,32}... | collective-permute-start | bytes 442376 | tf_op jit(solution)/shard_map/ppermute | solution.py:370
  24.9 11.2 %collective-permute-start = (f32[12,24,128]{2,1,0:T(8,128)S(1)}, f32[12,24,128]{2,1,0:T(8,128)S(1)}, u32[]{:S(2)}, u32[]{:S(2)}) collective-permute-start(f32[12,24,128]{2,1,0:T(8,128)S(1)} %get-tuple-element.20), channel_id=1, source_target_pairs={{0,4},{4,8},{8,12},{12,16},{16,20},{20,24},{24,28},{28,32},{32,36}... | collective-permute-start | bytes 442376 | tf_op jit(solution)/shard_map/ppermute | solution.py:369
  26.8 9.3 %copy-start = (bf16[768,384]{1,0:T(8,128)(2,1)S(1)}, bf16[768,384]{1,0:T(8,128)(2,1)}, u32[]{:S(2)}) copy-start(bf16[768,384]{1,0:T(8,128)(2,1)} %constant.6.clone.weights_ref) | copy-start | bytes 1769476

commit v6 on v5

--- a/solution.py
+++ b/solution.py
@@ -24,6 +24,7 @@
 
 PLANES = 4
 CHUNKS = 16
+SHIFT = 2
 VMEM_LIMIT = 24 * 1024 * 1024
 
 
@@ -160,7 +161,7 @@
 
 
 def flow_kernel(weights_ref, own_ref, low_ref, high_ref, out_ref, fields, middle, slopes, lifted):
-    for ref, count, base in ((low_ref, 3, 0), (own_ref, 4, 12), (high_ref, 3, 28)):
+    for ref, count, base in ((low_ref, 4, 0), (own_ref, 4, 16), (high_ref, 2, 32)):
         for j in range(count):
             for g in range(4):
                 for r, row in enumerate(unpacked(ref[4 * j + g])):
@@ -366,14 +367,15 @@
     blocks = lax.axis_size(LONG_AXES)
     up = [(i, (i + 1) % blocks) for i in range(blocks)]
     own, lines = lax.optimization_barrier((own, line_owner.reshape(64, 128)))
-    low = lax.ppermute(own[4:16], LONG_AXES, up)
-    high = lax.ppermute(own[0:12], LONG_AXES, [(b, a) for a, b in up])
+    low = lax.ppermute(own, LONG_AXES, up)
+    high = lax.ppermute(own[0:8], LONG_AXES, [(b, a) for a, b in up])
     first = lax.axis_index("y").astype(jnp.int32).reshape(1)
     own, lower, place = lax.optimization_barrier((own, *slots(first, lines)))
     table = swap(flow(own, low, high), BLOCK_AXES)
     outgoing = gather(table, lower, place).reshape(32, 16, 128)
     record = swap(outgoing, LAST_AXES)
-    record = record.reshape(16, 2, 2, 8, 128).transpose(2, 1, 0, 3, 4).reshape(512, 128)
+    record = record.reshape(16, 2, 2, 8, 128).transpose(2, 1, 0, 3, 4).reshape(2, 256, 128)
+    record = jnp.roll(record, -SHIFT, 1).reshape(512, 128)
     return record[None, None]
 
 

time: 82.8 us -> 82.6 us (level)
  waiting for transfers between devices: 7.62 us -> 1.67 us
  blocking collectives: 52.4 us -> 57.9 us
    ppermute x2, waiting for transfers between devices: 7.62 us -> 1.67 us  [the longest x1 0.91 us: body(): low = lax.ppermute(own, LONG_AXES, up)]
    all_to_all x3, blocking collectives: 52.4 us -> 57.9 us  [swap(): return lax.all_to_all(x, axes, split_axis=0, concat_axis=0, tiled=True)]
  transfers between devices with their start and end apart: 2 -> 2, of which waited for: 1 -> 2; matrix products, arithmetic and copies ran while one was open for 0% -> 0% of each run, Pallas kernels for 2% -> 2%
where the time goes in v6:
time: 82.6 us; the launch traced here: 82.2 us
  blocking collectives  57.9 us (70%)
  starting transfers between devices  14.3 us (17%)
  Pallas kernels  7.48 us (9%)
  waiting for transfers between devices  1.67 us (2%)
    all_to_all x3, blocking collectives, swap(): return lax.all_to_all(x, axes, split_axis=0, concat_axis=0, tiled=True)  57.9 us
    ppermute x1, starting transfers between devices, body(): high = lax.ppermute(own[0:8], LONG_AXES, [(b, a) for a, b in up])  10.3 us
    ppermute x1, starting transfers between devices, body(): low = lax.ppermute(own, LONG_AXES, up)  3.95 us
    pallas_call x1, Pallas kernels, flow(): pl.pallas_call(flow_kernel, out_shape=pltpu.VMEM((16, 64, 128), jnp.float...  2.42 us
    pallas_call x1, Pallas kernels, gather(): pl.pallas_call(gather_kernel, out_shape=jax.ShapeDtypeStruct((16, 2, 16,...  2.37 us
    pallas_call x1, Pallas kernels, slots(): pl.pallas_call(slots_kernel, out_shape=(shape, shape), in_specs=[pl.Block...  1.66 us
  transfers between devices with their start and end apart: 2, of which 2 were waited for; matrix products, arithmetic and copies ran while one was open for 0% of the time, Pallas kernels for 2%

profile of v6, /device:TPU:6, one launch (start us, length us, event | category | flops | bytes accessed | tf_op | source)
XLA Modules:
  0.0 82.2 jit_solution(10618479348368398805)
XLA Ops:
  0.0 1.0 %pack.1 = f32[16,24,128]{2,1,0:T(8,128)S(1)} custom-call(f32[4,4,2048]{2,1,0:T(4,128)} %bitcast.14), custom_call_target="tpu_custom_call" | custom-call | flops 100000 | bytes 400000 | tf_op jit(solution)/shard_map/pack/pallas_call | solution.py:78
  1.0 11.6 %all_to_all.15.own_ref = f32[16,24,128]{2,1,0:T(8,128)S(1)} all-to-all(f32[16,24,128]{2,1,0:T(8,128)S(1)} %pack.1), channel_id=1, replica_groups=mesh['xl'=2,'co'=2,'xh'=2,'z'=16,'y'=4] {'y','xl','co'}, dimensions={0} | all-to-all | bytes 393216 | tf_op jit(solution)/shard_map/all_to_all | solution.py:362
  12.6 0.0 copy-start.1
  12.6 3.9 %collective-permute-start = (f32[16,24,128]{2,1,0:T(8,128)S(1)}, f32[16,24,128]{2,1,0:T(8,128)S(1)}, u32[]{:S(2)}, u32[]{:S(2)}) collective-permute-start(f32[16,24,128]{2,1,0:T(8,128)S(1)} %all_to_all.15.own_ref), channel_id=1, source_target_pairs={{0,4},{4,8},{8,12},{12,16},{16,20},{20,24},{24,28},{28,32},{32,36}... | collective-permute-start | bytes 589832 | tf_op jit(solution)/shard_map/ppermute | solution.py:370
  16.6 10.3 %collective-permute-start.1 = (f32[8,24,128]{2,1,0:T(8,128)S(1)}, f32[8,24,128]{2,1,0:T(8,128)S(1)}, u32[]{:S(2)}, u32[]{:S(2)}) collective-permute-start(f32[8,24,128]{2,1,0:T(8,128)S(1)} %slice.11), channel_id=1, source_target_pairs={{4,0},{8,4},{12,8},{16,12},{20,16},{24,20},{28,24},{32,28},{36,32}... | collective-permute-start | bytes 294920 | tf_op jit(solution)/shard_map/ppermute | solution.py:371
  26.9 0.0 copy-done.1
  26.9 0.0 copy-start
  27.0 1.7 %slots.1 = (f32[2,4,8,128]{3,2,1,0:T(8,128)S(1)}, f32[2,4,8,128]{3,2,1,0:T(8,128)S(1)}) custom-call(s32[1]{0:T(128)} %bitcast.2.first_ref, s32[64,128]{1,0:T(8,128)S(1)} %bitcast.10), custom_call_target="tpu_custom_call" | custom-call | flops 600000000 | bytes 100000 | tf_op jit(solution)/shard_map/slots/pallas_call | solution.py:305
  28.6 0.8 collective-permute-done.1.high_ref
  29.4 0.9 %collective-permute-done.low_ref = f32[16,24,128]{2,1,0:T(8,128)S(1)} collective-permute-done((f32[16,24,128]{2,1,0:T(8,128)S(1)}, f32[16,24,128]{2,1,0:T(8,128)S(1)}, u32[]{:S(2)}, u32[]{:S(2)}) %collective-permute-start) | collective-permute-done | bytes 196640 | tf_op jit(solution)/shard_map/ppermute | solution.py:370
  30.3 0.0 copy-done
  30.3 2.4 %flow.1 = f32[16,64,128]{2,1,0:T(8,128)S(1)} custom-call(bf16[768,384]{1,0:T(8,128)(2,1)S(1)} %copy-done, f32[16,24,128]{2,1,0:T(8,128)S(1)} %all_to_all.15.own_ref, f32[16,24,128]{2,1,0:T(8,128)S(1)} %collective-permute-done.low_ref, f32[8,24,128]{2,1,0:T(8,128)S(1)} %collective-permute-done.1.high_ref), custom_call_target="tpu_custom_call" | custom-call | flops 30000000 | bytes 1000000 | tf_op jit(solution)/shard_map/flow/pallas_call | solution.py:254
  32.7 13.5 %all_to_all.16.table_ref = f32[16,64,128]{2,1,0:T(8,128)S(1)} all-to-all(f32[16,64,128]{2,1,0:T(8,128)S(1)} %flow.1), channel_id=1, replica_groups=mesh['xl'=2,'co'=2,'xh'=2,'z'=16,'y'=4] {'y','xl','co'}, dimensions={0} | all-to-all | bytes 1048576 | tf_op jit(solution)/shard_map/all_to_all | solution.py:362
  46.2 2.4 %gather.1 = f32[16,2,16,128]{3,2,1,0:T(8,128)S(1)} custom-call(f32[16,64,128]{2,1,0:T(8,128)S(1)} %all_to_all.16.table_ref, f32[2,4,8,128]{3,2,1,0:T(8,128)S(1)} %get-tuple-element.17.lower_ref, f32[2,4,8,128]{3,2,1,0:T(8,128)S(1)} %get-tuple-element.18.place_ref), custom_call_target="tpu_custom_call" | custom-call | flops 2200000000 | bytes 1000000 | tf_op jit(solution)/shard_map/gather/pallas_call | solution.py:350
  48.6 32.9 %all_to_all.17 = f32[32,16,128]{2,1,0:T(8,128)S(1)} all-to-all(f32[32,16,128]{2,1,0:T(8,128)S(1)} %bitcast.9), channel_id=1, replica_groups=mesh['xl'=2,'co'=2,'xh'=2,'z'=16,'y'=4] {'z','xh'}, dimensions={0} | all-to-all | bytes 524288 | tf_op jit(solution)/shard_map/all_to_all | solution.py:362
  81.5 0.7 pad_maximum_fusion
  (4 shorter events, 0.1 us)
Async XLA Ops:
  12.6 14.3 %copy-start.1 = (s32[8192,1]{0,1:T(1,128)S(1)}, s32[8192,1]{0,1:T(1,128)}, u32[]{:S(2)}) copy-start(s32[8192,1]{0,1:T(1,128)} %param.4) | copy-start | bytes 98308
  12.6 17.7 %collective-permute-start = (f32[16,24,128]{2,1,0:T(8,128)S(1)}, f32[16,24,128]{2,1,0:T(8,128)S(1)}, u32[]{:S(2)}, u32[]{:S(2)}) collective-permute-start(f32[16,24,128]{2,1,0:T(8,128)S(1)} %all_to_all.15.own_ref), channel_id=1, source_target_pairs={{0,4},{4,8},{8,12},{12,16},{16,20},{20,24},{24,28},{28,32},{32,36}... | collective-permute-start | bytes 589832 | tf_op jit(solution)/shard_map/ppermute | solution.py:370
  16.6 12.8 %collective-permute-start.1 = (f32[8,24,128]{2,1,0:T(8,128)S(1)}, f32[8,24,128]{2,1,0:T(8,128)S(1)}, u32[]{:S(2)}, u32[]{:S(2)}) collective-permute-start(f32[8,24,128]{2,1,0:T(8,128)S(1)} %slice.11), channel_id=1, source_target_pairs={{4,0},{8,4},{12,8},{16,12},{20,16},{24,20},{28,24},{32,28},{36,32}... | collective-permute-start | bytes 294920 | tf_op jit(solution)/shard_map/ppermute | solution.py:371
  26.9 3.3 %copy-start = (bf16[768,384]{1,0:T(8,128)(2,1)S(1)}, bf16[768,384]{1,0:T(8,128)(2,1)}, u32[]{:S(2)}) copy-start(bf16[768,384]{1,0:T(8,128)(2,1)} %constant.6.clone.weights_ref) | copy-start | bytes 1769476

commit v7 on v6

--- a/solution.py
+++ b/solution.py
@@ -7,7 +7,7 @@
 from jax.sharding import Mesh
 from jax.sharding import PartitionSpec as P
 
-BLOCK_AXES = ("y", "xl", "co")
+BLOCK_AXES = ("xl", "y", "co")
 LONG_AXES = ("xh", "z")
 LAST_AXES = ("z", "xh")
 
@@ -160,11 +160,20 @@
     return d_x, d_y, d_z, lap
 
 
+def place(g, j, count=4):
+    sizes = {"xl": 2, "y": count, "co": 2}
+    index = {"xl": g // 2, "y": j, "co": g % 2}
+    at = 0
+    for axis in BLOCK_AXES:
+        at = at * sizes[axis] + index[axis]
+    return at
+
+
 def flow_kernel(weights_ref, own_ref, low_ref, high_ref, out_ref, fields, middle, slopes, lifted):
     for ref, count, base in ((low_ref, 4, 0), (own_ref, 4, 16), (high_ref, 2, 32)):
         for j in range(count):
             for g in range(4):
-                for r, row in enumerate(unpacked(ref[4 * j + g])):
+                for r, row in enumerate(unpacked(ref[place(g, j, count)])):
                     fields[g, base + 4 * j + r] = row
 
     plane = lax.broadcasted_iota(jnp.int32, (4, 8, 128), 1) % 4
@@ -227,10 +236,10 @@
             rows = rows * scale
             energy[pair] = rows * rows if g == 0 else energy[pair] + rows * rows
             for copy in range(4):
-                out_ref[4 * copy + g, 8 * pair : 8 * pair + 8, :] = rows
+                out_ref[place(g, copy), 8 * pair : 8 * pair + 8, :] = rows
     for pair in range(8):
         for copy in range(4):
-            out_ref[4 * copy + 3, 8 * pair : 8 * pair + 8, :] = energy[pair]
+            out_ref[place(3, copy), 8 * pair : 8 * pair + 8, :] = energy[pair]
 
 
 def filter_taps(ring):
@@ -368,7 +377,7 @@
     up = [(i, (i + 1) % blocks) for i in range(blocks)]
     own, lines = lax.optimization_barrier((own, line_owner.reshape(64, 128)))
     low = lax.ppermute(own, LONG_AXES, up)
-    high = lax.ppermute(own[0:8], LONG_AXES, [(b, a) for a, b in up])
+    high = lax.ppermute(own.reshape(2, 4, 2, 24, 128)[:, 0:2].reshape(8, 24, 128), LONG_AXES, [(b, a) for a, b in up])
     first = lax.axis_index("y").astype(jnp.int32).reshape(1)
     own, lower, place = lax.optimization_barrier((own, *slots(first, lines)))
     table = swap(flow(own, low, high), BLOCK_AXES)

time: 82.6 us -> 82.2 us (level)
  no operation moved by 1% of the time
where the time goes in v7:
time: 82.2 us; the launch traced here: 81.8 us
  blocking collectives  57.9 us (70%)
  starting transfers between devices  14.2 us (17%)
  Pallas kernels  7.5 us (9%)
  waiting for transfers between devices  1.37 us (2%)
    all_to_all x3, blocking collectives, swap(): return lax.all_to_all(x, axes, split_axis=0, concat_axis=0, tiled=True)  57.9 us
    ppermute x1, starting transfers between devices, body(): lax.ppermute(own.reshape(2, 4, 2, 24, 128)[:, 0:2].reshape(8, 24, 128), L...  10.3 us
    ppermute x1, starting transfers between devices, body(): low = lax.ppermute(own, LONG_AXES, up)  3.81 us
    pallas_call x1, Pallas kernels, flow(): pl.pallas_call(flow_kernel, out_shape=pltpu.VMEM((16, 64, 128), jnp.float...  2.42 us
    pallas_call x1, Pallas kernels, gather(): pl.pallas_call(gather_kernel, out_shape=jax.ShapeDtypeStruct((16, 2, 16,...  2.37 us
    pallas_call x1, Pallas kernels, slots(): pl.pallas_call(slots_kernel, out_shape=(shape, shape), in_specs=[pl.Block...  1.68 us
  transfers between devices with their start and end apart: 2, of which 2 were waited for; matrix products, arithmetic and copies ran while one was open for 0% of the time, Pallas kernels for 2%

profile of v7, /device:TPU:6, one launch (start us, length us, event | category | flops | bytes accessed | tf_op | source)
XLA Modules:
  0.0 81.8 jit_solution(4485924431332816769)
XLA Ops:
  0.0 1.0 %pack.1 = f32[16,24,128]{2,1,0:T(8,128)S(1)} custom-call(f32[4,4,2048]{2,1,0:T(4,128)} %bitcast.17), custom_call_target="tpu_custom_call" | custom-call | flops 100000 | bytes 400000 | tf_op jit(solution)/shard_map/pack/pallas_call | solution.py:78
  1.0 11.8 %all_to_all.15.own_ref = f32[16,24,128]{2,1,0:T(8,128)S(1)} all-to-all(f32[16,24,128]{2,1,0:T(8,128)S(1)} %pack.1), channel_id=1, replica_groups=mesh['xl'=2,'co'=2,'xh'=2,'z'=16,'y'=4] {'xl','y','co'}, dimensions={0} | all-to-all | bytes 393216 | tf_op jit(solution)/shard_map/all_to_all | solution.py:371
  12.9 3.8 %collective-permute-start = (f32[16,24,128]{2,1,0:T(8,128)S(1)}, f32[16,24,128]{2,1,0:T(8,128)S(1)}, u32[]{:S(2)}, u32[]{:S(2)}) collective-permute-start(f32[16,24,128]{2,1,0:T(8,128)S(1)} %all_to_all.15.own_ref), channel_id=1, source_target_pairs={{0,4},{4,8},{8,12},{12,16},{16,20},{20,24},{24,28},{28,32},{32,36}... | collective-permute-start | bytes 589832 | tf_op jit(solution)/shard_map/ppermute | solution.py:379
  16.7 0.0 copy-start.1
  16.7 10.3 %collective-permute-start.1 = (f32[8,24,128]{2,1,0:T(8,128)S(1)}, f32[8,24,128]{2,1,0:T(8,128)S(1)}, u32[]{:S(2)}, u32[]{:S(2)}) collective-permute-start(f32[8,24,128]{2,1,0:T(8,128)S(1)} %bitcast.18), channel_id=1, source_target_pairs={{4,0},{8,4},{12,8},{16,12},{20,16},{24,20},{28,24},{32,28},{36,32}... | collective-permute-start | bytes 294920 | tf_op jit(solution)/shard_map/ppermute | solution.py:380
  27.1 0.0 copy-done.1
  27.1 0.0 copy-start
  27.1 1.7 %slots.1 = (f32[2,4,8,128]{3,2,1,0:T(8,128)S(1)}, f32[2,4,8,128]{3,2,1,0:T(8,128)S(1)}) custom-call(s32[1]{0:T(128)} %bitcast.2.first_ref, s32[64,128]{1,0:T(8,128)S(1)} %bitcast.13), custom_call_target="tpu_custom_call" | custom-call | flops 600000000 | bytes 100000 | tf_op jit(solution)/shard_map/slots/pallas_call | solution.py:314
  28.8 0.5 collective-permute-done.1.high_ref
  29.3 0.9 %collective-permute-done.low_ref = f32[16,24,128]{2,1,0:T(8,128)S(1)} collective-permute-done((f32[16,24,128]{2,1,0:T(8,128)S(1)}, f32[16,24,128]{2,1,0:T(8,128)S(1)}, u32[]{:S(2)}, u32[]{:S(2)}) %collective-permute-start) | collective-permute-done | bytes 196640 | tf_op jit(solution)/shard_map/ppermute | solution.py:379
  30.2 0.0 copy-done
  30.2 2.4 %flow.1 = f32[16,64,128]{2,1,0:T(8,128)S(1)} custom-call(bf16[768,384]{1,0:T(8,128)(2,1)S(1)} %copy-done, f32[16,24,128]{2,1,0:T(8,128)S(1)} %all_to_all.15.own_ref, f32[16,24,128]{2,1,0:T(8,128)S(1)} %collective-permute-done.low_ref, f32[8,24,128]{2,1,0:T(8,128)S(1)} %collective-permute-done.1.high_ref), custom_call_target="tpu_custom_call" | custom-call | flops 30000000 | bytes 1000000 | tf_op jit(solution)/shard_map/flow/pallas_call | solution.py:263
  32.6 13.2 %all_to_all.16.table_ref = f32[16,64,128]{2,1,0:T(8,128)S(1)} all-to-all(f32[16,64,128]{2,1,0:T(8,128)S(1)} %flow.1), channel_id=1, replica_groups=mesh['xl'=2,'co'=2,'xh'=2,'z'=16,'y'=4] {'xl','y','co'}, dimensions={0} | all-to-all | bytes 1048576 | tf_op jit(solution)/shard_map/all_to_all | solution.py:371
  45.8 2.4 %gather.1 = f32[16,2,16,128]{3,2,1,0:T(8,128)S(1)} custom-call(f32[16,64,128]{2,1,0:T(8,128)S(1)} %all_to_all.16.table_ref, f32[2,4,8,128]{3,2,1,0:T(8,128)S(1)} %get-tuple-element.17.lower_ref, f32[2,4,8,128]{3,2,1,0:T(8,128)S(1)} %get-tuple-element.18.place_ref), custom_call_target="tpu_custom_call" | custom-call | flops 2200000000 | bytes 1000000 | tf_op jit(solution)/shard_map/gather/pallas_call | solution.py:359
  48.2 32.9 %all_to_all.17 = f32[32,16,128]{2,1,0:T(8,128)S(1)} all-to-all(f32[32,16,128]{2,1,0:T(8,128)S(1)} %bitcast.12), channel_id=1, replica_groups=mesh['xl'=2,'co'=2,'xh'=2,'z'=16,'y'=4] {'z','xh'}, dimensions={0} | all-to-all | bytes 524288 | tf_op jit(solution)/shard_map/all_to_all | solution.py:371
  81.1 0.7 pad_maximum_fusion
  (4 shorter events, 0.1 us)
Async XLA Ops:
  12.9 17.3 %collective-permute-start = (f32[16,24,128]{2,1,0:T(8,128)S(1)}, f32[16,24,128]{2,1,0:T(8,128)S(1)}, u32[]{:S(2)}, u32[]{:S(2)}) collective-permute-start(f32[16,24,128]{2,1,0:T(8,128)S(1)} %all_to_all.15.own_ref), channel_id=1, source_target_pairs={{0,4},{4,8},{8,12},{12,16},{16,20},{20,24},{24,28},{28,32},{32,36}... | collective-permute-start | bytes 589832 | tf_op jit(solution)/shard_map/ppermute | solution.py:379
  16.7 10.4 %copy-start.1 = (s32[8192,1]{0,1:T(1,128)S(1)}, s32[8192,1]{0,1:T(1,128)}, u32[]{:S(2)}) copy-start(s32[8192,1]{0,1:T(1,128)} %param.4) | copy-start | bytes 98308
  16.7 12.5 %collective-permute-start.1 = (f32[8,24,128]{2,1,0:T(8,128)S(1)}, f32[8,24,128]{2,1,0:T(8,128)S(1)}, u32[]{:S(2)}, u32[]{:S(2)}) collective-permute-start(f32[8,24,128]{2,1,0:T(8,128)S(1)} %bitcast.18), channel_id=1, source_target_pairs={{4,0},{8,4},{12,8},{16,12},{20,16},{24,20},{28,24},{32,28},{36,32}... | collective-permute-start | bytes 294920 | tf_op jit(solution)/shard_map/ppermute | solution.py:380
  27.1 3.1 %copy-start = (bf16[768,384]{1,0:T(8,128)(2,1)S(1)}, bf16[768,384]{1,0:T(8,128)(2,1)}, u32[]{:S(2)}) copy-start(bf16[768,384]{1,0:T(8,128)(2,1)} %constant.6.clone.weights_ref) | copy-start | bytes 1769476

commit v8 on v7

--- a/solution.py
+++ b/solution.py
@@ -193,7 +193,7 @@
             middle[g, pl.ds(4 * i, 4)] = (u, v, w)[g] + time_step * tend
         return carry
 
-    lax.fori_loop(0, 8, first, 0, unroll=4)
+    lax.fori_loop(0, 8, first, 0, unroll=8)
 
     def second(i, carry):
         low = 4 + 4 * i
@@ -206,7 +206,7 @@
             lifted[g, pl.ds(4 * i, 4)] = s
         return carry
 
-    lax.fori_loop(0, 6, second, 0, unroll=3)
+    lax.fori_loop(0, 6, second, 0, unroll=6)
 
     sub = lax.broadcasted_iota(jnp.int32, (8, 128), 0)
     odd_z, first_row = sub % 2 == 1, sub < 4

time: 82.2 us -> 81.8 us (level)
  no operation moved by 1% of the time
where the time goes in v8:
time: 81.8 us; the launch traced here: 81.5 us
  blocking collectives  58 us (71%)
  starting transfers between devices  14.2 us (17%)
  Pallas kernels  7.15 us (9%)
  waiting for transfers between devices  1.37 us (2%)
    all_to_all x3, blocking collectives, swap(): return lax.all_to_all(x, axes, split_axis=0, concat_axis=0, tiled=True)  58 us
    ppermute x1, starting transfers between devices, body(): lax.ppermute(own.reshape(2, 4, 2, 24, 128)[:, 0:2].reshape(8, 24, 128), L...  10.3 us
    ppermute x1, starting transfers between devices, body(): low = lax.ppermute(own, LONG_AXES, up)  3.81 us
    pallas_call x1, Pallas kernels, gather(): pl.pallas_call(gather_kernel, out_shape=jax.ShapeDtypeStruct((16, 2, 16,...  2.37 us
    pallas_call x1, Pallas kernels, flow(): pl.pallas_call(flow_kernel, out_shape=pltpu.VMEM((16, 64, 128), jnp.float...  2.07 us
    pallas_call x1, Pallas kernels, slots(): pl.pallas_call(slots_kernel, out_shape=(shape, shape), in_specs=[pl.Block...  1.68 us
  transfers between devices with their start and end apart: 2, of which 2 were waited for; matrix products, arithmetic and copies ran while one was open for 0% of the time, Pallas kernels for 2%

profile of v8, /device:TPU:6, one launch (start us, length us, event | category | flops | bytes accessed | tf_op | source)
XLA Modules:
  0.0 81.5 jit_solution(8851658511144315293)
XLA Ops:
  0.0 1.0 %pack.1 = f32[16,24,128]{2,1,0:T(8,128)S(1)} custom-call(f32[4,4,2048]{2,1,0:T(4,128)} %bitcast.17), custom_call_target="tpu_custom_call" | custom-call | flops 100000 | bytes 400000 | tf_op jit(solution)/shard_map/pack/pallas_call | solution.py:78
  1.0 11.8 %all_to_all.15.own_ref = f32[16,24,128]{2,1,0:T(8,128)S(1)} all-to-all(f32[16,24,128]{2,1,0:T(8,128)S(1)} %pack.1), channel_id=1, replica_groups=mesh['xl'=2,'co'=2,'xh'=2,'z'=16,'y'=4] {'xl','y','co'}, dimensions={0} | all-to-all | bytes 393216 | tf_op jit(solution)/shard_map/all_to_all | solution.py:371
  12.9 3.8 %collective-permute-start = (f32[16,24,128]{2,1,0:T(8,128)S(1)}, f32[16,24,128]{2,1,0:T(8,128)S(1)}, u32[]{:S(2)}, u32[]{:S(2)}) collective-permute-start(f32[16,24,128]{2,1,0:T(8,128)S(1)} %all_to_all.15.own_ref), channel_id=1, source_target_pairs={{0,4},{4,8},{8,12},{12,16},{16,20},{20,24},{24,28},{28,32},{32,36}... | collective-permute-start | bytes 589832 | tf_op jit(solution)/shard_map/ppermute | solution.py:379
  16.7 0.0 copy-start.1
  16.7 10.3 %collective-permute-start.1 = (f32[8,24,128]{2,1,0:T(8,128)S(1)}, f32[8,24,128]{2,1,0:T(8,128)S(1)}, u32[]{:S(2)}, u32[]{:S(2)}) collective-permute-start(f32[8,24,128]{2,1,0:T(8,128)S(1)} %bitcast.18), channel_id=1, source_target_pairs={{4,0},{8,4},{12,8},{16,12},{20,16},{24,20},{28,24},{32,28},{36,32}... | collective-permute-start | bytes 294920 | tf_op jit(solution)/shard_map/ppermute | solution.py:380
  27.1 0.0 copy-done.1
  27.1 0.0 copy-start
  27.1 1.7 %slots.1 = (f32[2,4,8,128]{3,2,1,0:T(8,128)S(1)}, f32[2,4,8,128]{3,2,1,0:T(8,128)S(1)}) custom-call(s32[1]{0:T(128)} %bitcast.2.first_ref, s32[64,128]{1,0:T(8,128)S(1)} %bitcast.13), custom_call_target="tpu_custom_call" | custom-call | flops 600000000 | bytes 100000 | tf_op jit(solution)/shard_map/slots/pallas_call | solution.py:314
  28.8 0.5 collective-permute-done.1.high_ref
  29.3 0.9 %collective-permute-done.low_ref = f32[16,24,128]{2,1,0:T(8,128)S(1)} collective-permute-done((f32[16,24,128]{2,1,0:T(8,128)S(1)}, f32[16,24,128]{2,1,0:T(8,128)S(1)}, u32[]{:S(2)}, u32[]{:S(2)}) %collective-permute-start) | collective-permute-done | bytes 196640 | tf_op jit(solution)/shard_map/ppermute | solution.py:379
  30.2 0.0 copy-done
  30.2 2.1 %flow.1 = f32[16,64,128]{2,1,0:T(8,128)S(1)} custom-call(bf16[768,384]{1,0:T(8,128)(2,1)S(1)} %copy-done, f32[16,24,128]{2,1,0:T(8,128)S(1)} %all_to_all.15.own_ref, f32[16,24,128]{2,1,0:T(8,128)S(1)} %collective-permute-done.low_ref, f32[8,24,128]{2,1,0:T(8,128)S(1)} %collective-permute-done.1.high_ref), custom_call_target="tpu_custom_call" | custom-call | flops 30000000 | bytes 1000000 | tf_op jit(solution)/shard_map/flow/pallas_call | solution.py:263
  32.2 13.2 %all_to_all.16.table_ref = f32[16,64,128]{2,1,0:T(8,128)S(1)} all-to-all(f32[16,64,128]{2,1,0:T(8,128)S(1)} %flow.1), channel_id=1, replica_groups=mesh['xl'=2,'co'=2,'xh'=2,'z'=16,'y'=4] {'xl','y','co'}, dimensions={0} | all-to-all | bytes 1048576 | tf_op jit(solution)/shard_map/all_to_all | solution.py:371
  45.4 2.4 %gather.1 = f32[16,2,16,128]{3,2,1,0:T(8,128)S(1)} custom-call(f32[16,64,128]{2,1,0:T(8,128)S(1)} %all_to_all.16.table_ref, f32[2,4,8,128]{3,2,1,0:T(8,128)S(1)} %get-tuple-element.17.lower_ref, f32[2,4,8,128]{3,2,1,0:T(8,128)S(1)} %get-tuple-element.18.place_ref), custom_call_target="tpu_custom_call" | custom-call | flops 2200000000 | bytes 1000000 | tf_op jit(solution)/shard_map/gather/pallas_call | solution.py:359
  47.8 32.9 %all_to_all.17 = f32[32,16,128]{2,1,0:T(8,128)S(1)} all-to-all(f32[32,16,128]{2,1,0:T(8,128)S(1)} %bitcast.12), channel_id=1, replica_groups=mesh['xl'=2,'co'=2,'xh'=2,'z'=16,'y'=4] {'z','xh'}, dimensions={0} | all-to-all | bytes 524288 | tf_op jit(solution)/shard_map/all_to_all | solution.py:371
  80.8 0.7 pad_maximum_fusion
  (4 shorter events, 0.1 us)
Async XLA Ops:
  12.9 17.3 %collective-permute-start = (f32[16,24,128]{2,1,0:T(8,128)S(1)}, f32[16,24,128]{2,1,0:T(8,128)S(1)}, u32[]{:S(2)}, u32[]{:S(2)}) collective-permute-start(f32[16,24,128]{2,1,0:T(8,128)S(1)} %all_to_all.15.own_ref), channel_id=1, source_target_pairs={{0,4},{4,8},{8,12},{12,16},{16,20},{20,24},{24,28},{28,32},{32,36}... | collective-permute-start | bytes 589832 | tf_op jit(solution)/shard_map/ppermute | solution.py:379
  16.7 10.4 %copy-start.1 = (s32[8192,1]{0,1:T(1,128)S(1)}, s32[8192,1]{0,1:T(1,128)}, u32[]{:S(2)}) copy-start(s32[8192,1]{0,1:T(1,128)} %param.4) | copy-start | bytes 98308
  16.7 12.5 %collective-permute-start.1 = (f32[8,24,128]{2,1,0:T(8,128)S(1)}, f32[8,24,128]{2,1,0:T(8,128)S(1)}, u32[]{:S(2)}, u32[]{:S(2)}) collective-permute-start(f32[8,24,128]{2,1,0:T(8,128)S(1)} %bitcast.18), channel_id=1, source_target_pairs={{4,0},{8,4},{12,8},{16,12},{20,16},{24,20},{28,24},{32,28},{36,32}... | collective-permute-start | bytes 294920 | tf_op jit(solution)/shard_map/ppermute | solution.py:380
  27.1 3.1 %copy-start = (bf16[768,384]{1,0:T(8,128)(2,1)S(1)}, bf16[768,384]{1,0:T(8,128)(2,1)}, u32[]{:S(2)}) copy-start(bf16[768,384]{1,0:T(8,128)(2,1)} %constant.6.clone.weights_ref) | copy-start | bytes 1769476

commit v9 on v8

--- a/solution.py
+++ b/solution.py
@@ -40,7 +40,12 @@
     return pl.CostEstimate(flops=flops, bytes_accessed=moved, transcendentals=0)
 
 
-def pack_kernel(x_ref, out_ref):
+def pack_kernel(far_ref, out_ref, x_ref, arrived):
+    copies = [pltpu.make_async_copy(far_ref.at[z], x_ref.at[z], arrived.at[z]) for z in range(PLANES)]
+    for copy in copies:
+        copy.start()
+    for copy in copies:
+        copy.wait()
     lane = lanes_of((8, 128))
     rows = [[x_ref[:, r, 128 * c : 128 * c + 128] for r in range(4)] for c in range(CHUNKS)]
     for c in range(CHUNKS):
@@ -78,8 +83,9 @@
     return pl.pallas_call(
         pack_kernel,
         out_shape=pltpu.VMEM((CHUNKS, 24, 128), jnp.float32),
-        in_specs=whole(1),
+        in_specs=[pl.BlockSpec(memory_space=pl.ANY)],
         out_specs=whole(1)[0],
+        scratch_shapes=[pltpu.VMEM((PLANES, 4, 2048), jnp.float32), pltpu.SemaphoreType.DMA((PLANES,))],
         cost_estimate=cost(100_000, 400_000),
         name="pack",
     )(x)

time: 81.8 us -> 81.8 us (level)
  no operation moved by 1% of the time
where the time goes in v9:
time: 81.8 us; the launch traced here: 81.4 us
  blocking collectives  58 us (71%)
  starting transfers between devices  14.2 us (17%)
  Pallas kernels  7.05 us (9%)
  waiting for transfers between devices  1.39 us (2%)
    all_to_all x3, blocking collectives, swap(): return lax.all_to_all(x, axes, split_axis=0, concat_axis=0, tiled=True)  58 us
    ppermute x1, starting transfers between devices, body(): lax.ppermute(own.reshape(2, 4, 2, 24, 128)[:, 0:2].reshape(8, 24, 128), L...  10.3 us
    ppermute x1, starting transfers between devices, body(): low = lax.ppermute(own, LONG_AXES, up)  3.81 us
    pallas_call x1, Pallas kernels, gather(): pl.pallas_call(gather_kernel, out_shape=jax.ShapeDtypeStruct((16, 2, 16,...  2.37 us
    pallas_call x1, Pallas kernels, flow(): pl.pallas_call(flow_kernel, out_shape=pltpu.VMEM((16, 64, 128), jnp.float...  2.06 us
    pallas_call x1, Pallas kernels, slots(): pl.pallas_call(slots_kernel, out_shape=(shape, shape), in_specs=[pl.Block...  1.66 us
  transfers between devices with their start and end apart: 2, of which 2 were waited for; matrix products, arithmetic and copies ran while one was open for 0% of the time, Pallas kernels for 2%

profile of v9, /device:TPU:6, one launch (start us, length us, event | category | flops | bytes accessed | tf_op | source)
XLA Modules:
  0.0 81.4 jit_solution(7237547589172002402)
XLA Ops:
  0.0 1.0 %pack.1 = f32[16,24,128]{2,1,0:T(8,128)S(1)} custom-call(f32[4,4,2048]{2,1,0:T(4,128)} %bitcast.17), custom_call_target="tpu_custom_call" | custom-call | flops 100000 | bytes 400000 | tf_op jit(solution)/shard_map/pack/pallas_call | solution.py:83
  1.0 11.8 %all_to_all.15.own_ref = f32[16,24,128]{2,1,0:T(8,128)S(1)} all-to-all(f32[16,24,128]{2,1,0:T(8,128)S(1)} %pack.1), channel_id=1, replica_groups=mesh['xl'=2,'co'=2,'xh'=2,'z'=16,'y'=4] {'xl','y','co'}, dimensions={0} | all-to-all | bytes 393216 | tf_op jit(solution)/shard_map/all_to_all | solution.py:377
  12.8 3.8 %collective-permute-start = (f32[16,24,128]{2,1,0:T(8,128)S(1)}, f32[16,24,128]{2,1,0:T(8,128)S(1)}, u32[]{:S(2)}, u32[]{:S(2)}) collective-permute-start(f32[16,24,128]{2,1,0:T(8,128)S(1)} %all_to_all.15.own_ref), channel_id=1, source_target_pairs={{0,4},{4,8},{8,12},{12,16},{16,20},{20,24},{24,28},{28,32},{32,36}... | collective-permute-start | bytes 589832 | tf_op jit(solution)/shard_map/ppermute | solution.py:385
  16.6 0.0 copy-start.1
  16.7 10.3 %collective-permute-start.1 = (f32[8,24,128]{2,1,0:T(8,128)S(1)}, f32[8,24,128]{2,1,0:T(8,128)S(1)}, u32[]{:S(2)}, u32[]{:S(2)}) collective-permute-start(f32[8,24,128]{2,1,0:T(8,128)S(1)} %bitcast.18), channel_id=1, source_target_pairs={{4,0},{8,4},{12,8},{16,12},{20,16},{24,20},{28,24},{32,28},{36,32}... | collective-permute-start | bytes 294920 | tf_op jit(solution)/shard_map/ppermute | solution.py:386
  27.0 0.0 copy-done.1
  27.0 0.0 copy-start
  27.0 1.7 %slots.1 = (f32[2,4,8,128]{3,2,1,0:T(8,128)S(1)}, f32[2,4,8,128]{3,2,1,0:T(8,128)S(1)}) custom-call(s32[1]{0:T(128)} %bitcast.2.first_ref, s32[64,128]{1,0:T(8,128)S(1)} %bitcast.13), custom_call_target="tpu_custom_call" | custom-call | flops 600000000 | bytes 100000 | tf_op jit(solution)/shard_map/slots/pallas_call | solution.py:320
  28.7 0.5 collective-permute-done.1.high_ref
  29.2 0.9 %collective-permute-done.low_ref = f32[16,24,128]{2,1,0:T(8,128)S(1)} collective-permute-done((f32[16,24,128]{2,1,0:T(8,128)S(1)}, f32[16,24,128]{2,1,0:T(8,128)S(1)}, u32[]{:S(2)}, u32[]{:S(2)}) %collective-permute-start) | collective-permute-done | bytes 196640 | tf_op jit(solution)/shard_map/ppermute | solution.py:385
  30.1 0.0 copy-done
  30.1 2.1 %flow.1 = f32[16,64,128]{2,1,0:T(8,128)S(1)} custom-call(bf16[768,384]{1,0:T(8,128)(2,1)S(1)} %copy-done, f32[16,24,128]{2,1,0:T(8,128)S(1)} %all_to_all.15.own_ref, f32[16,24,128]{2,1,0:T(8,128)S(1)} %collective-permute-done.low_ref, f32[8,24,128]{2,1,0:T(8,128)S(1)} %collective-permute-done.1.high_ref), custom_call_target="tpu_custom_call" | custom-call | flops 30000000 | bytes 1000000 | tf_op jit(solution)/shard_map/flow/pallas_call | solution.py:269
  32.2 13.2 %all_to_all.16.table_ref = f32[16,64,128]{2,1,0:T(8,128)S(1)} all-to-all(f32[16,64,128]{2,1,0:T(8,128)S(1)} %flow.1), channel_id=1, replica_groups=mesh['xl'=2,'co'=2,'xh'=2,'z'=16,'y'=4] {'xl','y','co'}, dimensions={0} | all-to-all | bytes 1048576 | tf_op jit(solution)/shard_map/all_to_all | solution.py:377
  45.4 2.4 %gather.1 = f32[16,2,16,128]{3,2,1,0:T(8,128)S(1)} custom-call(f32[16,64,128]{2,1,0:T(8,128)S(1)} %all_to_all.16.table_ref, f32[2,4,8,128]{3,2,1,0:T(8,128)S(1)} %get-tuple-element.17.lower_ref, f32[2,4,8,128]{3,2,1,0:T(8,128)S(1)} %get-tuple-element.18.place_ref), custom_call_target="tpu_custom_call" | custom-call | flops 2200000000 | bytes 1000000 | tf_op jit(solution)/shard_map/gather/pallas_call | solution.py:365
  47.8 32.9 %all_to_all.17 = f32[32,16,128]{2,1,0:T(8,128)S(1)} all-to-all(f32[32,16,128]{2,1,0:T(8,128)S(1)} %bitcast.12), channel_id=1, replica_groups=mesh['xl'=2,'co'=2,'xh'=2,'z'=16,'y'=4] {'z','xh'}, dimensions={0} | all-to-all | bytes 524288 | tf_op jit(solution)/shard_map/all_to_all | solution.py:377
  80.7 0.7 pad_maximum_fusion
  (4 shorter events, 0.1 us)
Async XLA Ops:
  12.8 17.3 %collective-permute-start = (f32[16,24,128]{2,1,0:T(8,128)S(1)}, f32[16,24,128]{2,1,0:T(8,128)S(1)}, u32[]{:S(2)}, u32[]{:S(2)}) collective-permute-start(f32[16,24,128]{2,1,0:T(8,128)S(1)} %all_to_all.15.own_ref), channel_id=1, source_target_pairs={{0,4},{4,8},{8,12},{12,16},{16,20},{20,24},{24,28},{28,32},{32,36}... | collective-permute-start | bytes 589832 | tf_op jit(solution)/shard_map/ppermute | solution.py:385
  16.6 10.4 %copy-start.1 = (s32[8192,1]{0,1:T(1,128)S(1)}, s32[8192,1]{0,1:T(1,128)}, u32[]{:S(2)}) copy-start(s32[8192,1]{0,1:T(1,128)} %param.4) | copy-start | bytes 98308
  16.7 12.5 %collective-permute-start.1 = (f32[8,24,128]{2,1,0:T(8,128)S(1)}, f32[8,24,128]{2,1,0:T(8,128)S(1)}, u32[]{:S(2)}, u32[]{:S(2)}) collective-permute-start(f32[8,24,128]{2,1,0:T(8,128)S(1)} %bitcast.18), channel_id=1, source_target_pairs={{4,0},{8,4},{12,8},{16,12},{20,16},{24,20},{28,24},{32,28},{36,32}... | collective-permute-start | bytes 294920 | tf_op jit(solution)/shard_map/ppermute | solution.py:386
  27.0 3.1 %copy-start = (bf16[768,384]{1,0:T(8,128)(2,1)S(1)}, bf16[768,384]{1,0:T(8,128)(2,1)}, u32[]{:S(2)}) copy-start(bf16[768,384]{1,0:T(8,128)(2,1)} %constant.6.clone.weights_ref) | copy-start | bytes 1769476
